TPU v7x, 32 devices: a whole 2x2x4 slice. The times are simulated.
32 devices in a mesh: groups: 2 (over x), gx: 16 (over z, y, core).
Axes of the slice: x: 2, y: 2, z: 4, core: 2. Of those that a mesh axis runs over, the one named last changes fastest.
Arguments:
- tokens: bfloat16 [4096, 1536], P(('groups', 'gx')), parts along dimension 0, may hold values from -6 to 6
- upstream: bfloat16 [4096, 1536], P(('groups', 'gx')), parts along dimension 0, may hold values from -6 to 6
- sample_of_token: int32 [4096], P(('groups', 'gx')), parts along dimension 0, may hold values from 0 to 15, never falling along the last dimension, each value on 1 to 256 neighbouring positions
- reward_level: int32 [32], P('groups'), parts along dimension 0, may hold values from 0 to 15
- up_weight: bfloat16 [6144, 1536], P('gx'), may hold values from -0.15625 to 0.15625
- down_weight: bfloat16 [6144, 1536], P('gx'), may hold values from -0.078125 to 0.078125
Outputs:
- grad_tokens: bfloat16 [4096, 1536], P(('groups', 'gx')), parts along dimension 0
- grad_up: float32 [12288, 1536], P(('groups', 'gx')), parts along dimension 0
- grad_down: float32 [12288, 1536], P(('groups', 'gx')), parts along dimension 0
There are 2 independent parts, one for each index of `groups`. A program takes and returns all parts, laid end to end along the dimension named above; an argument that names none is the same for every part. Nothing has to cross between parts.
All inputs are finite; a program needn't handle non-finite values.
Results may differ from a plain program's by a relative error of at most 0.006.
Values may be sent and summed in bfloat16 or wider, within the bound.
No kernel may reach another device: no remote copies, remote signals or barrier semaphores. Data moves between devices by JAX's collectives and lax.ppermute only.
A program may use at most 128 MiB of HBM per device.

v0:
```python
import jax
import jax.numpy as jnp
from jax import lax
from jax.sharding import PartitionSpec as P

LEVELS = 16


def partner(block, axis, bit):
    count = lax.axis_size(axis)
    route = []
    for low in range(count):
        high = low | 1 << bit
        if high != low and high < count:
            route += [(low, high), (high, low)]
    return lax.ppermute(block, axis, route)


def gelu_value(v):
    inner = 0.7978845608 * (v + 0.044715 * v * v * v)
    return 0.5 * v * (1.0 + jnp.tanh(inner))


def gelu_slope(v):
    inner = 0.7978845608 * (v + 0.044715 * v * v * v)
    hyper = jnp.tanh(inner)
    return 0.5 * (1.0 + hyper) + 0.5 * v * (1.0 - hyper * hyper) * 0.7978845608 * (
        1.0 + 3.0 * 0.044715 * v * v
    )


def collect(piece, bit_list, position, swapper):
    for bit in bit_list:
        upper = position >> bit & 1 == 1
        other = swapper(piece, bit)
        first = jnp.where(upper, other, piece)
        second = jnp.where(upper, piece, other)
        piece = jnp.concatenate([first, second], axis=1)
    return piece


def spread(piece, bit_list, position, swapper):
    for bit in reversed(bit_list):
        half = piece.shape[1] // 2
        lower = piece[:, :half]
        higher = piece[:, half:]
        upper = position >> bit & 1 == 1
        keep = jnp.where(upper, higher, lower)
        send = jnp.where(upper, lower, higher)
        piece = keep + swapper(send, bit)
    return piece


def swap_tokens(value, bit):
    return partner(value, "gx", bit)


def swap_units(value, bit):
    return partner(value, "gx", bit)


def swap_unit_sums(value, bit):
    return partner(value, "gx", bit)


def swap_token_sums(value, bit):
    return partner(value, "gx", bit)


def local(tokens, upstream, sample_of_token, reward_level, up_weight, down_weight):
    sample_count = reward_level.shape[0]
    matches = sample_of_token[:, None] == jnp.arange(sample_count, dtype=jnp.int32)[None, :]
    level = jnp.sum(jnp.where(matches, reward_level[None, :], 0), axis=1)
    weight = (level + 1).astype(jnp.float32) / LEVELS
    weighted = (weight[:, None] * upstream.astype(jnp.float32)).astype(jnp.bfloat16)
    bit_total = lax.axis_size("gx").bit_length() - 1
    low_count = bit_total // 2
    low_bits = list(range(low_count))
    high_bits = list(range(low_count, bit_total))
    token_bits, unit_bits = (low_bits, high_bits)
    position = lax.axis_index("gx")
    acts = collect(jnp.stack([tokens, weighted]), token_bits, position, swap_tokens)
    x_rows = acts[0]
    g_rows = acts[1]
    mats = collect(jnp.stack([up_weight, down_weight]), unit_bits, position, swap_units)
    up_rows = mats[0]
    down_rows = mats[1]
    last_last = (((1,), (1,)), ((), ()))
    first_first = (((0,), (0,)), ((), ()))
    pre = lax.dot_general(x_rows, up_rows, last_last, preferred_element_type=jnp.float32)
    hidden = gelu_value(pre).astype(jnp.bfloat16)
    grad_hidden = lax.dot_general(g_rows, down_rows, last_last, preferred_element_type=jnp.float32)
    grad_pre = (grad_hidden * gelu_slope(pre)).astype(jnp.bfloat16)
    down_part = lax.dot_general(hidden, g_rows, first_first, preferred_element_type=jnp.float32)
    up_part = lax.dot_general(grad_pre, x_rows, first_first, preferred_element_type=jnp.float32)
    grads = spread(jnp.stack([up_part, down_part]), unit_bits, position, swap_unit_sums)
    token_part = jnp.dot(grad_pre, up_rows, preferred_element_type=jnp.float32)
    token_sum = spread(token_part[None], token_bits, position, swap_token_sums)[0]
    grad_tokens = (weighted.astype(jnp.float32) + token_sum).astype(jnp.bfloat16)
    return (grad_tokens, grads[0], grads[1])


def solution(mesh):
    return jax.shard_map(
        local,
        mesh=mesh,
        in_specs=(
            P(("groups", "gx"), None),
            P(("groups", "gx"), None),
            P(("groups", "gx")),
            P("groups"),
            P("gx", None),
            P("gx", None),
        ),
        out_specs=(P(("groups", "gx"), None), P(("groups", "gx"), None), P(("groups", "gx"), None)),
        check_vma=False,
    )
```

profile of v0, /device:TPU:0, one launch (start us, length us, event | category | flops | bytes accessed | tf_op | source)
XLA Modules:
  0.0 807.2 jit_solution(12887107064663471179)
XLA Ops:
  0.7 1.9 pad_maximum_fusion.3
  2.6 3.1 collective-permute-start.2
  5.8 51.3 %collective-permute-done.2 = bf16[2,384,1536]{2,1,0:T(8,128)(2,1)} collective-permute-done((bf16[2,384,1536]{2,1,0:T(8,128)(2,1)S(1)}, bf16[2,384,1536]{2,1,0:T(8,128)(2,1)}, u32[]{:S(2)}, u32[]{:S(2)}) %collective-permute-start.2) | collective-permute-done | bytes 2359328 | tf_op jit(solution)/shard_map/ppermute | solution.py:16
  57.0 2.3 broadcast_select_fusion.4
  59.4 2.4 pad_maximum_fusion.2
  62.3 2.8 collective-permute-start.3
  65.2 0.9 pad_maximum_fusion.6
  66.2 2.6 collective-permute-done
  68.8 1.3 broadcast_select_fusion.8
  71.0 1.2 pad_maximum_fusion.5
  72.2 1.5 collective-permute-start.1
  73.8 35.2 %collective-permute-done.1 = bf16[2,256,1536]{2,1,0:T(8,128)(2,1)} collective-permute-done((bf16[2,256,1536]{2,1,0:T(8,128)(2,1)}, bf16[2,256,1536]{2,1,0:T(8,128)(2,1)}, u32[]{:S(2)}, u32[]{:S(2)}) %collective-permute-start.1) | collective-permute-done | bytes 1572896 | tf_op jit(solution)/shard_map/ppermute | solution.py:16
  109.0 2.2 broadcast_select_fusion.6
  111.2 156.4 %collective-permute-done.3 = bf16[2,768,1536]{2,1,0:T(8,128)(2,1)} collective-permute-done((bf16[2,768,1536]{2,1,0:T(8,128)(2,1)}, bf16[2,768,1536]{2,1,0:T(8,128)(2,1)}, u32[]{:S(2)}, u32[]{:S(2)}) %collective-permute-start.3) | collective-permute-done | bytes 4718624 | tf_op jit(solution)/shard_map/ppermute | solution.py:16
  267.6 3.4 broadcast_select_fusion.2
  271.1 2.6 fusion.26
  273.7 1.0 copy-done.5
  274.8 3.9 fusion.14
  278.7 2.9 convolution_bitcast_fusion
  281.6 2.7 convolution_bitcast_fusion.1
  284.3 2.3 broadcast_select_fusion
  286.6 407.1 %collective-permute-done.6 = f32[2,768,1536]{2,1,0:T(8,128)} collective-permute-done((f32[2,768,1536]{2,1,0:T(8,128)S(1)}, f32[2,768,1536]{2,1,0:T(8,128)}, u32[]{:S(2)}, u32[]{:S(2)}) %collective-permute-start.6) | collective-permute-done | bytes 9437216 | tf_op jit(solution)/shard_map/ppermute | solution.py:16
  693.8 6.1 select_add_fusion
  699.9 1.0 slice_select_fusion
  701.3 4.4 convolution_bitcast_fusion.2
  706.0 1.3 collective-permute-start.4
  707.3 33.4 %collective-permute-done.4 = f32[1,256,1536]{2,1,0:T(8,128)S(1)} collective-permute-done((f32[1,256,1536]{2,1,0:T(8,128)S(1)}, f32[1,256,1536]{2,1,0:T(8,128)S(1)}, u32[]{:S(2)}, u32[]{:S(2)}) %collective-permute-start.4) | collective-permute-done | bytes 1572896 | tf_op jit(solution)/shard_map/ppermute | solution.py:16
  741.3 2.3 collective-permute-done.5
  743.6 1.0 fusion.24
  744.6 58.5 %collective-permute-done.7 = f32[2,384,1536]{2,1,0:T(8,128)S(1)} collective-permute-done((f32[2,384,1536]{2,1,0:T(8,128)S(1)}, f32[2,384,1536]{2,1,0:T(8,128)S(1)}, u32[]{:S(2)}, u32[]{:S(2)}) %collective-permute-start.7) | collective-permute-done | bytes 4718624 | tf_op jit(solution)/shard_map/ppermute | solution.py:16
  803.0 1.6 select_add_fusion.1
  804.7 2.5 slice_bitcast_fusion
  (35 shorter events, 2.9 us)
Async XLA Ops:
  0.6 56.4 %copy-start.3 = (bf16[384,1536]{1,0:T(8,128)(2,1)S(1)}, bf16[384,1536]{1,0:T(8,128)(2,1)}, u32[]{:S(2)}) copy-start(bf16[384,1536]{1,0:T(8,128)(2,1)} %param.11) | copy-start | bytes 3538948
  0.6 5.0 copy-start.9
  0.7 5.0 copy-start.10
  2.6 54.4 %collective-permute-start.2 = (bf16[2,384,1536]{2,1,0:T(8,128)(2,1)S(1)}, bf16[2,384,1536]{2,1,0:T(8,128)(2,1)}, u32[]{:S(2)}, u32[]{:S(2)}) collective-permute-start(bf16[2,384,1536]{2,1,0:T(8,128)(2,1)S(1)} %pad_maximum_fusion.3), channel_id=1, source_target_pairs={{0,4},{4,0},{1,5},{5,1},{2,6},{6,2},{3,7},{7,3},{8,12},{12,8},{9,1... | collective-permute-start | bytes 7077896 | tf_op jit(solution)/shard_map/ppermute | solution.py:16
  59.3 3.0 copy-start
  59.3 5.7 copy-start.7
  59.4 5.8 copy-start.6
  62.3 205.3 %collective-permute-start.3 = (bf16[2,768,1536]{2,1,0:T(8,128)(2,1)}, bf16[2,768,1536]{2,1,0:T(8,128)(2,1)}, u32[]{:S(2)}, u32[]{:S(2)}) collective-permute-start(bf16[2,768,1536]{2,1,0:T(8,128)(2,1)} %pad_maximum_fusion.2), channel_id=1, source_target_pairs={{0,8},{8,0},{1,9},{9,1},{2,10},{10,2},{3,11},{11,3},{4,12},{12,4},... | collective-permute-start | bytes 14155784 | tf_op jit(solution)/shard_map/ppermute | solution.py:16
  66.2 2.6 collective-permute-start
  70.1 0.9 copy-start.2
  72.2 36.8 %collective-permute-start.1 = (bf16[2,256,1536]{2,1,0:T(8,128)(2,1)}, bf16[2,256,1536]{2,1,0:T(8,128)(2,1)}, u32[]{:S(2)}, u32[]{:S(2)}) collective-permute-start(bf16[2,256,1536]{2,1,0:T(8,128)(2,1)} %pad_maximum_fusion.5), channel_id=1, source_target_pairs={{0,2},{2,0},{1,3},{3,1},{4,6},{6,4},{5,7},{7,5},{8,10},{10,8},{9,1... | collective-permute-start | bytes 4718600 | tf_op jit(solution)/shard_map/ppermute | solution.py:16
  73.8 193.9 %copy-start.1 = (bf16[2,384,1536]{2,1,0:T(8,128)(2,1)S(1)}, bf16[2,384,1536]{2,1,0:T(8,128)(2,1)}, u32[]{:S(2)}) copy-start(bf16[2,384,1536]{2,1,0:T(8,128)(2,1)} %copy-done) | copy-start | bytes 7077892
  271.1 2.7 copy-start.4
  271.1 3.7 copy-start.5
  278.7 2.9 copy-start.11
  286.6 407.2 %collective-permute-start.6 = (f32[2,768,1536]{2,1,0:T(8,128)S(1)}, f32[2,768,1536]{2,1,0:T(8,128)}, u32[]{:S(2)}, u32[]{:S(2)}) collective-permute-start(f32[2,768,1536]{2,1,0:T(8,128)S(1)} %broadcast_select_fusion), channel_id=1, source_target_pairs={{0,8},{8,0},{1,9},{9,1},{2,10},{10,2},{3,11},{11,3},{4,12},{12,4},... | collective-permute-start | bytes 28311560 | tf_op jit(solution)/shard_map/ppermute | solution.py:16
  699.9 1.4 copy-start.12
  700.9 102.1 %collective-permute-start.7 = (f32[2,384,1536]{2,1,0:T(8,128)S(1)}, f32[2,384,1536]{2,1,0:T(8,128)S(1)}, u32[]{:S(2)}, u32[]{:S(2)}) collective-permute-start(f32[2,384,1536]{2,1,0:T(8,128)S(1)} %slice_select_fusion), channel_id=1, source_target_pairs={{0,4},{4,0},{1,5},{5,1},{2,6},{6,2},{3,7},{7,3},{8,12},{12,8},{9,1... | collective-permute-start | bytes 14155784 | tf_op jit(solution)/shard_map/ppermute | solution.py:16
  706.0 37.6 %copy-start.8 = (bf16[128,1536]{1,0:T(8,128)(2,1)S(1)}, bf16[128,1536]{1,0:T(8,128)(2,1)}, u32[]{:S(2)}) copy-start(bf16[128,1536]{1,0:T(8,128)(2,1)} %param.7) | copy-start | bytes 1179652
  706.0 34.7 %collective-permute-start.4 = (f32[1,256,1536]{2,1,0:T(8,128)S(1)}, f32[1,256,1536]{2,1,0:T(8,128)S(1)}, u32[]{:S(2)}, u32[]{:S(2)}) collective-permute-start(f32[1,256,1536]{2,1,0:T(8,128)S(1)} %slice_select_fusion.1), channel_id=1, source_target_pairs={{0,2},{2,0},{1,3},{3,1},{4,6},{6,4},{5,7},{7,5},{8,10},{10,8},{9,1... | collective-permute-start | bytes 4718600 | tf_op jit(solution)/shard_map/ppermute | solution.py:16
  741.3 2.4 collective-permute-start.5
where the time goes:
time: 807 us
  waiting for transfers between devices  747 us (93%)
  other arithmetic  28.8 us (4%)
  matrix products  16.6 us (2%)
  starting transfers between devices  8.86 us (1%)
    ppermute x8, waiting for transfers between devices, partner(): return lax.ppermute(block, axis, route)  747 us
  transfers between devices with their start and end apart: 8, of which 8 were waited for; matrix products, arithmetic and copies ran while one was open for 1% of the time, Pallas kernels for 0%

commit v1 on v0

v1 whole, which is shorter than its diff:
```python
import jax
import jax.numpy as jnp
from jax import lax
from jax.sharding import PartitionSpec as P

LEVELS = 16
LAST = (((1,), (1,)), ((), ()))
FIRST = (((0,), (0,)), ((), ()))


def ring_order(chips):
    if chips <= 8:
        return list(range(0, chips, 2)) + list(range(1, chips, 2))[::-1]
    return list(range(chips))


def ring_route(count):
    order = ring_order(count // 2)
    chips = len(order)
    route = []
    for place in range(chips):
        here = order[place]
        route.append((2 * here, 2 * order[(place + 1) % chips]))
        route.append((2 * here + 1, 2 * order[(place - 1) % chips] + 1))
    return route


def gelu_pair(v):
    inner = 0.7978845608 * (v + 0.044715 * v * v * v)
    hyper = jnp.tanh(inner)
    value = 0.5 * v * (1.0 + hyper)
    slope = 0.5 * (1.0 + hyper) + 0.5 * v * (1.0 - hyper * hyper) * 0.7978845608 * (
        1.0 + 3.0 * 0.044715 * v * v
    )
    return value, slope


def dot(a, b, dims):
    return lax.dot_general(a, b, dims, preferred_element_type=jnp.float32)


def local(tokens, upstream, sample_of_token, reward_level, up_weight, down_weight):
    count = lax.axis_size("gx")
    chips = count // 2
    route = ring_route(count)
    swap = [(i, i ^ 1) for i in range(count)]

    def hop(block):
        return lax.ppermute(block, "gx", route)

    def across(block):
        return lax.ppermute(block, "gx", swap)

    matches = sample_of_token[:, None] == jnp.arange(reward_level.shape[0], dtype=jnp.int32)[None, :]
    level = jnp.sum(jnp.where(matches, reward_level[None, :], 0), axis=1)
    weight = (level + 1).astype(jnp.float32) / LEVELS
    weighted = (weight[:, None] * upstream.astype(jnp.float32)).astype(jnp.bfloat16)

    units = up_weight.shape[0]
    up_rows = jnp.concatenate([up_weight, across(up_weight)], axis=0)
    down_rows = jnp.concatenate([down_weight, across(down_weight)], axis=0)

    x, g = tokens, weighted
    xs, gs, hs, ps = [], [], [], []
    carried = None
    own_part = None
    for step in range(chips):
        if step:
            x, g = hop(x), hop(g)
        pre = dot(x, up_rows, LAST)
        value, slope = gelu_pair(pre)
        hidden = value.astype(jnp.bfloat16)
        grad_pre = (dot(g, down_rows, LAST) * slope).astype(jnp.bfloat16)
        xs.append(x)
        gs.append(g)
        hs.append(hidden)
        ps.append(grad_pre)
        part = dot(grad_pre, up_rows, (((1,), (0,)), ((), ())))
        if step == 0:
            own_part = part
        else:
            total = part if carried is None else part + carried.astype(jnp.float32)
            carried = hop(total.astype(jnp.bfloat16))
    grad_tokens = (
        weighted.astype(jnp.float32) + own_part + carried.astype(jnp.float32)
    ).astype(jnp.bfloat16)

    x_all, g_all = jnp.concatenate(xs), jnp.concatenate(gs)
    h_all, p_all = jnp.concatenate(hs), jnp.concatenate(ps)
    up_other = across(dot(p_all[:, units:], x_all, FIRST).astype(jnp.bfloat16))
    down_other = across(dot(h_all[:, units:], g_all, FIRST).astype(jnp.bfloat16))
    grad_up = dot(p_all[:, :units], x_all, FIRST) + up_other.astype(jnp.float32)
    grad_down = dot(h_all[:, :units], g_all, FIRST) + down_other.astype(jnp.float32)
    return grad_tokens, grad_up, grad_down


def solution(mesh):
    rows = P(("groups", "gx"), None)
    return jax.shard_map(
        local,
        mesh=mesh,
        in_specs=(rows, rows, P(("groups", "gx")), P("groups"), P("gx", None), P("gx", None)),
        out_specs=(rows, rows, rows),
        check_vma=False,
    )
```

time: 807 us -> 111 us (0.14)
  waiting for transfers between devices: 747 us -> 41.4 us
  starting transfers between devices: 8.86 us -> 36.4 us
  other arithmetic: 28.8 us -> 1.89 us
  matrix products: 16.6 us -> 28.2 us
    ppermute x8 -> x25, waiting for transfers between devices: 747 us -> 41.4 us  [the longest x21 41.4 us: hop(): return lax.ppermute(block, 'gx', route)]
    ppermute x8 -> x25, starting transfers between devices: 8.86 us -> 36.4 us  [the longest x21 35.7 us: hop(): return lax.ppermute(block, 'gx', route)]
    select_n x8 -> x0, other arithmetic: 12.8 us -> none  [the longest x4 9.24 us: collect(): first = jnp.where(upper, other, piece)]
    dot_general x5 -> x28, matrix products: 16.6 us -> 28.2 us  [dot(): return lax.dot_general(a, b, dims, preferred_element_type=jnp.float32)]
    add x3 -> x0, other arithmetic: 8.19 us -> none  [spread(): piece = keep + swapper(send, bit)]
  transfers between devices with their start and end apart: 8 -> 25, of which waited for: 8 -> 17; matrix products, arithmetic and copies ran while one was open for 1% -> 28% of each run, Pallas kernels for 0% -> 0%
where the time goes in v1:
time: 111 us
  waiting for transfers between devices  41.4 us (37%)
  starting transfers between devices  36.4 us (33%)
  matrix products  28.2 us (25%)
  local copies, waits for them, and re-layouts  2.01 us (2%)
  other arithmetic  1.89 us (2%)
    ppermute x21, waiting for transfers between devices, hop(): return lax.ppermute(block, 'gx', route)  41.4 us
    ppermute x21, starting transfers between devices, hop(): return lax.ppermute(block, 'gx', route)  35.7 us
    dot_general x28, matrix products, dot(): return lax.dot_general(a, b, dims, preferred_element_type=jnp.float32)  28.2 us
  transfers between devices with their start and end apart: 25, of which 17 were waited for; matrix products, arithmetic and copies ran while one was open for 28% of the time, Pallas kernels for 0%

profile of v1, /device:TPU:0, one launch (start us, length us, event | category | flops | bytes accessed | tf_op | source)
XLA Modules:
  0.0 110.9 jit_solution(15688522593325153376)
XLA Ops:
  1.2 2.6 %collective-permute-start.9 = (bf16[128,1536]{1,0:T(8,128)(2,1)}, bf16[128,1536]{1,0:T(8,128)(2,1)S(1)}, u32[]{:S(2)}, u32[]{:S(2)}) collective-permute-start(bf16[128,1536]{1,0:T(8,128)(2,1)} %param.6), channel_id=1, source_target_pairs={{0,4},{1,3},{4,8},{5,1},{8,12},{9,5},{12,14},{13,9},{14,10},{15,13... | collective-permute-start | bytes 1179656 | tf_op jit(solution)/shard_map/ppermute | solution.py:49
  5.7 1.6 %collective-permute-start.2 = (bf16[128,1536]{1,0:T(8,128)(2,1)S(1)}, bf16[128,1536]{1,0:T(8,128)(2,1)S(1)}, u32[]{:S(2)}, u32[]{:S(2)}) collective-permute-start(bf16[128,1536]{1,0:T(8,128)(2,1)S(1)} %get-tuple-element.4), channel_id=1, source_target_pairs={{0,4},{1,3},{4,8},{5,1},{8,12},{9,5},{12,14},{13,9},{14,10},{15,13... | collective-permute-start | bytes 1179656 | tf_op jit(solution)/shard_map/ppermute | solution.py:49
  9.7 2.1 %collective-permute-start.10 = (bf16[128,1536]{1,0:T(8,128)(2,1)S(1)}, bf16[128,1536]{1,0:T(8,128)(2,1)S(1)}, u32[]{:S(2)}, u32[]{:S(2)}) collective-permute-start(bf16[128,1536]{1,0:T(8,128)(2,1)S(1)} %collective-permute-done.9), channel_id=1, source_target_pairs={{0,4},{1,3},{4,8},{5,1},{8,12},{9,5},{12,14},{13,9},{14,10},{15,13... | collective-permute-start | bytes 1179656 | tf_op jit(solution)/shard_map/ppermute | solution.py:49
  11.8 2.1 %collective-permute-done.2 = bf16[128,1536]{1,0:T(8,128)(2,1)S(1)} collective-permute-done((bf16[128,1536]{1,0:T(8,128)(2,1)S(1)}, bf16[128,1536]{1,0:T(8,128)(2,1)S(1)}, u32[]{:S(2)}, u32[]{:S(2)}) %collective-permute-start.2) | collective-permute-done | bytes 393248 | tf_op jit(solution)/shard_map/ppermute | solution.py:49
  13.9 2.1 %collective-permute-start.3 = (bf16[128,1536]{1,0:T(8,128)(2,1)S(1)}, bf16[128,1536]{1,0:T(8,128)(2,1)S(1)}, u32[]{:S(2)}, u32[]{:S(2)}) collective-permute-start(bf16[128,1536]{1,0:T(8,128)(2,1)S(1)} %collective-permute-done.2), channel_id=1, source_target_pairs={{0,4},{1,3},{4,8},{5,1},{8,12},{9,5},{12,14},{13,9},{14,10},{15,13... | collective-permute-start | bytes 1179656 | tf_op jit(solution)/shard_map/ppermute | solution.py:49
  16.1 2.1 %collective-permute-done.10 = bf16[128,1536]{1,0:T(8,128)(2,1)S(1)} collective-permute-done((bf16[128,1536]{1,0:T(8,128)(2,1)S(1)}, bf16[128,1536]{1,0:T(8,128)(2,1)S(1)}, u32[]{:S(2)}, u32[]{:S(2)}) %collective-permute-start.10) | collective-permute-done | bytes 393248 | tf_op jit(solution)/shard_map/ppermute | solution.py:49
  18.1 2.1 %collective-permute-start.11 = (bf16[128,1536]{1,0:T(8,128)(2,1)S(1)}, bf16[128,1536]{1,0:T(8,128)(2,1)S(1)}, u32[]{:S(2)}, u32[]{:S(2)}) collective-permute-start(bf16[128,1536]{1,0:T(8,128)(2,1)S(1)} %collective-permute-done.10), channel_id=1, source_target_pairs={{0,4},{1,3},{4,8},{5,1},{8,12},{9,5},{12,14},{13,9},{14,10},{15,13... | collective-permute-start | bytes 1179656 | tf_op jit(solution)/shard_map/ppermute | solution.py:49
  20.2 2.1 %collective-permute-done.3 = bf16[128,1536]{1,0:T(8,128)(2,1)S(1)} collective-permute-done((bf16[128,1536]{1,0:T(8,128)(2,1)S(1)}, bf16[128,1536]{1,0:T(8,128)(2,1)S(1)}, u32[]{:S(2)}, u32[]{:S(2)}) %collective-permute-start.3) | collective-permute-done | bytes 393248 | tf_op jit(solution)/shard_map/ppermute | solution.py:49
  22.4 2.1 %collective-permute-start.4 = (bf16[128,1536]{1,0:T(8,128)(2,1)S(1)}, bf16[128,1536]{1,0:T(8,128)(2,1)S(1)}, u32[]{:S(2)}, u32[]{:S(2)}) collective-permute-start(bf16[128,1536]{1,0:T(8,128)(2,1)S(1)} %collective-permute-done.3), channel_id=1, source_target_pairs={{0,4},{1,3},{4,8},{5,1},{8,12},{9,5},{12,14},{13,9},{14,10},{15,13... | collective-permute-start | bytes 1179656 | tf_op jit(solution)/shard_map/ppermute | solution.py:49
  29.0 1.6 %collective-permute-start.16 = (bf16[128,1536]{1,0:T(8,128)(2,1)S(1)}, bf16[128,1536]{1,0:T(8,128)(2,1)S(1)}, u32[]{:S(2)}, u32[]{:S(2)}) collective-permute-start(bf16[128,1536]{1,0:T(8,128)(2,1)S(1)} %convolution_convert_fusion.2), channel_id=1, source_target_pairs={{0,4},{1,3},{4,8},{5,1},{8,12},{9,5},{12,14},{13,9},{14,10},{15,13... | collective-permute-start | bytes 1179656 | tf_op jit(solution)/shard_map/ppermute | solution.py:49
  31.6 1.6 %collective-permute-start.12 = (bf16[128,1536]{1,0:T(8,128)(2,1)S(1)}, bf16[128,1536]{1,0:T(8,128)(2,1)S(1)}, u32[]{:S(2)}, u32[]{:S(2)}) collective-permute-start(bf16[128,1536]{1,0:T(8,128)(2,1)S(1)} %collective-permute-done.11), channel_id=1, source_target_pairs={{0,4},{1,3},{4,8},{5,1},{8,12},{9,5},{12,14},{13,9},{14,10},{15,13... | collective-permute-start | bytes 1179656 | tf_op jit(solution)/shard_map/ppermute | solution.py:49
  34.2 1.6 %collective-permute-start.5 = (bf16[128,1536]{1,0:T(8,128)(2,1)S(1)}, bf16[128,1536]{1,0:T(8,128)(2,1)S(1)}, u32[]{:S(2)}, u32[]{:S(2)}) collective-permute-start(bf16[128,1536]{1,0:T(8,128)(2,1)S(1)} %collective-permute-done.4), channel_id=1, source_target_pairs={{0,4},{1,3},{4,8},{5,1},{8,12},{9,5},{12,14},{13,9},{14,10},{15,13... | collective-permute-start | bytes 1179656 | tf_op jit(solution)/shard_map/ppermute | solution.py:49
  38.9 2.1 %collective-permute-done.12 = bf16[128,1536]{1,0:T(8,128)(2,1)S(1)} collective-permute-done((bf16[128,1536]{1,0:T(8,128)(2,1)S(1)}, bf16[128,1536]{1,0:T(8,128)(2,1)S(1)}, u32[]{:S(2)}, u32[]{:S(2)}) %collective-permute-start.12) | collective-permute-done | bytes 393248 | tf_op jit(solution)/shard_map/ppermute | solution.py:49
  43.6 1.7 %collective-permute-done.5 = bf16[128,1536]{1,0:T(8,128)(2,1)S(1)} collective-permute-done((bf16[128,1536]{1,0:T(8,128)(2,1)S(1)}, bf16[128,1536]{1,0:T(8,128)(2,1)S(1)}, u32[]{:S(2)}, u32[]{:S(2)}) %collective-permute-start.5) | collective-permute-done | bytes 393248 | tf_op jit(solution)/shard_map/ppermute | solution.py:49
  47.8 1.6 %collective-permute-done.17 = bf16[128,1536]{1,0:T(8,128)(2,1)S(1)} collective-permute-done((bf16[128,1536]{1,0:T(8,128)(2,1)S(1)}, bf16[128,1536]{1,0:T(8,128)(2,1)S(1)}, u32[]{:S(2)}, u32[]{:S(2)}) %collective-permute-start.17) | collective-permute-done | bytes 393248 | tf_op jit(solution)/shard_map/ppermute | solution.py:49
  49.9 1.6 %collective-permute-start.18 = (bf16[128,1536]{1,0:T(8,128)(2,1)S(1)}, bf16[128,1536]{1,0:T(8,128)(2,1)S(1)}, u32[]{:S(2)}, u32[]{:S(2)}) collective-permute-start(bf16[128,1536]{1,0:T(8,128)(2,1)S(1)} %fusion.6), channel_id=1, source_target_pairs={{0,4},{1,3},{4,8},{5,1},{8,12},{9,5},{12,14},{13,9},{14,10},{15,13... | collective-permute-start | bytes 1179656 | tf_op jit(solution)/shard_map/ppermute | solution.py:49
  51.6 2.1 %collective-permute-done.13 = bf16[128,1536]{1,0:T(8,128)(2,1)S(1)} collective-permute-done((bf16[128,1536]{1,0:T(8,128)(2,1)S(1)}, bf16[128,1536]{1,0:T(8,128)(2,1)S(1)}, u32[]{:S(2)}, u32[]{:S(2)}) %collective-permute-start.13) | collective-permute-done | bytes 393248 | tf_op jit(solution)/shard_map/ppermute | solution.py:49
  56.2 1.7 %collective-permute-done.6 = bf16[128,1536]{1,0:T(8,128)(2,1)S(1)} collective-permute-done((bf16[128,1536]{1,0:T(8,128)(2,1)S(1)}, bf16[128,1536]{1,0:T(8,128)(2,1)S(1)}, u32[]{:S(2)}, u32[]{:S(2)}) %collective-permute-start.6) | collective-permute-done | bytes 393248 | tf_op jit(solution)/shard_map/ppermute | solution.py:49
  60.5 1.6 %collective-permute-done.18 = bf16[128,1536]{1,0:T(8,128)(2,1)S(1)} collective-permute-done((bf16[128,1536]{1,0:T(8,128)(2,1)S(1)}, bf16[128,1536]{1,0:T(8,128)(2,1)S(1)}, u32[]{:S(2)}, u32[]{:S(2)}) %collective-permute-start.18) | collective-permute-done | bytes 393248 | tf_op jit(solution)/shard_map/ppermute | solution.py:49
  62.6 1.6 %collective-permute-start.19 = (bf16[128,1536]{1,0:T(8,128)(2,1)S(1)}, bf16[128,1536]{1,0:T(8,128)(2,1)S(1)}, u32[]{:S(2)}, u32[]{:S(2)}) collective-permute-start(bf16[128,1536]{1,0:T(8,128)(2,1)S(1)} %fusion.5), channel_id=1, source_target_pairs={{0,4},{1,3},{4,8},{5,1},{8,12},{9,5},{12,14},{13,9},{14,10},{15,13... | collective-permute-start | bytes 1179656 | tf_op jit(solution)/shard_map/ppermute | solution.py:49
  64.2 2.1 %collective-permute-done.14 = bf16[128,1536]{1,0:T(8,128)(2,1)S(1)} collective-permute-done((bf16[128,1536]{1,0:T(8,128)(2,1)S(1)}, bf16[128,1536]{1,0:T(8,128)(2,1)S(1)}, u32[]{:S(2)}, u32[]{:S(2)}) %collective-permute-start.14) | collective-permute-done | bytes 393248 | tf_op jit(solution)/shard_map/ppermute | solution.py:49
  68.8 1.7 %collective-permute-done.7 = bf16[128,1536]{1,0:T(8,128)(2,1)S(1)} collective-permute-done((bf16[128,1536]{1,0:T(8,128)(2,1)S(1)}, bf16[128,1536]{1,0:T(8,128)(2,1)S(1)}, u32[]{:S(2)}, u32[]{:S(2)}) %collective-permute-start.7) | collective-permute-done | bytes 393248 | tf_op jit(solution)/shard_map/ppermute | solution.py:49
  70.5 1.6 %collective-permute-start.8 = (bf16[128,1536]{1,0:T(8,128)(2,1)S(1)}, bf16[128,1536]{1,0:T(8,128)(2,1)S(1)}, u32[]{:S(2)}, u32[]{:S(2)}) collective-permute-start(bf16[128,1536]{1,0:T(8,128)(2,1)S(1)} %collective-permute-done.7), channel_id=1, source_target_pairs={{0,4},{1,3},{4,8},{5,1},{8,12},{9,5},{12,14},{13,9},{14,10},{15,13... | collective-permute-start | bytes 1179656 | tf_op jit(solution)/shard_map/ppermute | solution.py:49
  73.1 5.8 %collective-permute-done.15 = bf16[128,1536]{1,0:T(8,128)(2,1)S(1)} collective-permute-done((bf16[128,1536]{1,0:T(8,128)(2,1)S(1)}, bf16[128,1536]{1,0:T(8,128)(2,1)S(1)}, u32[]{:S(2)}, u32[]{:S(2)}) %collective-permute-start.15) | collective-permute-done | bytes 393248 | tf_op jit(solution)/shard_map/ppermute | solution.py:49
  79.9 3.3 %collective-permute-done.8 = bf16[128,1536]{1,0:T(8,128)(2,1)S(1)} collective-permute-done((bf16[128,1536]{1,0:T(8,128)(2,1)S(1)}, bf16[128,1536]{1,0:T(8,128)(2,1)S(1)}, u32[]{:S(2)}, u32[]{:S(2)}) %collective-permute-start.8) | collective-permute-done | bytes 393248 | tf_op jit(solution)/shard_map/ppermute | solution.py:49
  85.2 1.6 %collective-permute-start.20 = (bf16[128,1536]{1,0:T(8,128)(2,1)S(1)}, bf16[128,1536]{1,0:T(8,128)(2,1)S(1)}, u32[]{:S(2)}, u32[]{:S(2)}) collective-permute-start(bf16[128,1536]{1,0:T(8,128)(2,1)S(1)} %fusion.4), channel_id=1, source_target_pairs={{0,4},{1,3},{4,8},{5,1},{8,12},{9,5},{12,14},{13,9},{14,10},{15,13... | collective-permute-start | bytes 1179656 | tf_op jit(solution)/shard_map/ppermute | solution.py:49
  89.3 3.7 %collective-permute-done.20 = bf16[128,1536]{1,0:T(8,128)(2,1)S(1)} collective-permute-done((bf16[128,1536]{1,0:T(8,128)(2,1)S(1)}, bf16[128,1536]{1,0:T(8,128)(2,1)S(1)}, u32[]{:S(2)}, u32[]{:S(2)}) %collective-permute-start.20) | collective-permute-done | bytes 393248 | tf_op jit(solution)/shard_map/ppermute | solution.py:49
  93.5 1.6 %collective-permute-start.21 = (bf16[128,1536]{1,0:T(8,128)(2,1)S(1)}, bf16[128,1536]{1,0:T(8,128)(2,1)S(1)}, u32[]{:S(2)}, u32[]{:S(2)}) collective-permute-start(bf16[128,1536]{1,0:T(8,128)(2,1)S(1)} %fusion.3), channel_id=1, source_target_pairs={{0,4},{1,3},{4,8},{5,1},{8,12},{9,5},{12,14},{13,9},{14,10},{15,13... | collective-permute-start | bytes 1179656 | tf_op jit(solution)/shard_map/ppermute | solution.py:49
  95.1 6.2 %collective-permute-done.21 = bf16[128,1536]{1,0:T(8,128)(2,1)S(1)} collective-permute-done((bf16[128,1536]{1,0:T(8,128)(2,1)S(1)}, bf16[128,1536]{1,0:T(8,128)(2,1)S(1)}, u32[]{:S(2)}, u32[]{:S(2)}) %collective-permute-start.21) | collective-permute-done | bytes 393248 | tf_op jit(solution)/shard_map/ppermute | solution.py:49
  101.8 1.6 %collective-permute-start.22 = (bf16[128,1536]{1,0:T(8,128)(2,1)S(1)}, bf16[128,1536]{1,0:T(8,128)(2,1)S(1)}, u32[]{:S(2)}, u32[]{:S(2)}) collective-permute-start(bf16[128,1536]{1,0:T(8,128)(2,1)S(1)} %fusion.2), channel_id=1, source_target_pairs={{0,4},{1,3},{4,8},{5,1},{8,12},{9,5},{12,14},{13,9},{14,10},{15,13... | collective-permute-start | bytes 1179656 | tf_op jit(solution)/shard_map/ppermute | solution.py:49
  103.4 2.8 %convolution_add_fusion = f32[384,1536]{1,0:T(8,128)} fusion(bf16[1024,1536]{1,0:T(8,128)(2,1)S(1)} %constant_dynamic-update-slice_fusion.20, bf16[384,1536]{1,0:T(8,128)(2,1)S(1)} %collective-permute-done.24, bf16[1024,768]{1,0:T(8,128)(2,1)S(1)} %get-tuple-element.35), kind=kOutput, calls=%fused_computation | convolution fusion | flops 1209139200 | bytes 7471104 | tf_op jit(solution)/shard_map/dot_general | solution.py:39
  106.3 2.8 %convolution_add_fusion.1 = f32[384,1536]{1,0:T(8,128)} fusion(bf16[1024,1536]{1,0:T(8,128)(2,1)S(1)} %constant_dynamic-update-slice_fusion.12, bf16[384,1536]{1,0:T(8,128)(2,1)S(1)} %collective-permute-done.23, bf16[1024,768]{1,0:T(8,128)(2,1)S(1)} %get-tuple-element.19), kind=kOutput, calls=%fused_computation.1 | convolution fusion | flops 1209139200 | bytes 7471104 | tf_op jit(solution)/shard_map/dot_general | solution.py:39
  (72 shorter events, 37.1 us)
Async XLA Ops:
  0.6 8.1 %copy-start = (bf16[384,1536]{1,0:T(8,128)(2,1)S(1)}, bf16[384,1536]{1,0:T(8,128)(2,1)}, u32[]{:S(2)}) copy-start(bf16[384,1536]{1,0:T(8,128)(2,1)} %param.11) | copy-start | bytes 3538948
  0.6 23.9 %collective-permute-start.1 = (bf16[384,1536]{1,0:T(8,128)(2,1)}, bf16[384,1536]{1,0:T(8,128)(2,1)S(1)}, u32[]{:S(2)}, u32[]{:S(2)}) collective-permute-start(bf16[384,1536]{1,0:T(8,128)(2,1)} %param.10), channel_id=1, source_target_pairs={{0,1},{1,0},{2,3},{3,2},{4,5},{5,4},{6,7},{7,6},{8,9},{9,8},{10,11... | collective-permute-start | bytes 3538952 | tf_op jit(solution)/shard_map/ppermute | solution.py:52
  1.2 8.6 %collective-permute-start.9 = (bf16[128,1536]{1,0:T(8,128)(2,1)}, bf16[128,1536]{1,0:T(8,128)(2,1)S(1)}, u32[]{:S(2)}, u32[]{:S(2)}) collective-permute-start(bf16[128,1536]{1,0:T(8,128)(2,1)} %param.6), channel_id=1, source_target_pairs={{0,4},{1,3},{4,8},{5,1},{8,12},{9,5},{12,14},{13,9},{14,10},{15,13... | collective-permute-start | bytes 1179656 | tf_op jit(solution)/shard_map/ppermute | solution.py:49
  5.7 3.1 %copy-start.1 = (bf16[128,1536]{1,0:T(8,128)(2,1)S(1)}, bf16[128,1536]{1,0:T(8,128)(2,1)}, u32[]{:S(2)}) copy-start(bf16[128,1536]{1,0:T(8,128)(2,1)} %param.6) | copy-start | bytes 1179652
  5.7 8.2 %collective-permute-start.2 = (bf16[128,1536]{1,0:T(8,128)(2,1)S(1)}, bf16[128,1536]{1,0:T(8,128)(2,1)S(1)}, u32[]{:S(2)}, u32[]{:S(2)}) collective-permute-start(bf16[128,1536]{1,0:T(8,128)(2,1)S(1)} %get-tuple-element.4), channel_id=1, source_target_pairs={{0,4},{1,3},{4,8},{5,1},{8,12},{9,5},{12,14},{13,9},{14,10},{15,13... | collective-permute-start | bytes 1179656 | tf_op jit(solution)/shard_map/ppermute | solution.py:49
  7.3 18.2 %collective-permute-start = (bf16[384,1536]{1,0:T(8,128)(2,1)}, bf16[384,1536]{1,0:T(8,128)(2,1)S(1)}, u32[]{:S(2)}, u32[]{:S(2)}) collective-permute-start(bf16[384,1536]{1,0:T(8,128)(2,1)} %param.11), channel_id=1, source_target_pairs={{0,1},{1,0},{2,3},{3,2},{4,5},{5,4},{6,7},{7,6},{8,9},{9,8},{10,11... | collective-permute-start | bytes 3538952 | tf_op jit(solution)/shard_map/ppermute | solution.py:52
  9.7 8.4 %collective-permute-start.10 = (bf16[128,1536]{1,0:T(8,128)(2,1)S(1)}, bf16[128,1536]{1,0:T(8,128)(2,1)S(1)}, u32[]{:S(2)}, u32[]{:S(2)}) collective-permute-start(bf16[128,1536]{1,0:T(8,128)(2,1)S(1)} %collective-permute-done.9), channel_id=1, source_target_pairs={{0,4},{1,3},{4,8},{5,1},{8,12},{9,5},{12,14},{13,9},{14,10},{15,13... | collective-permute-start | bytes 1179656 | tf_op jit(solution)/shard_map/ppermute | solution.py:49
  13.9 8.4 %collective-permute-start.3 = (bf16[128,1536]{1,0:T(8,128)(2,1)S(1)}, bf16[128,1536]{1,0:T(8,128)(2,1)S(1)}, u32[]{:S(2)}, u32[]{:S(2)}) collective-permute-start(bf16[128,1536]{1,0:T(8,128)(2,1)S(1)} %collective-permute-done.2), channel_id=1, source_target_pairs={{0,4},{1,3},{4,8},{5,1},{8,12},{9,5},{12,14},{13,9},{14,10},{15,13... | collective-permute-start | bytes 1179656 | tf_op jit(solution)/shard_map/ppermute | solution.py:49
  18.1 13.4 %collective-permute-start.11 = (bf16[128,1536]{1,0:T(8,128)(2,1)S(1)}, bf16[128,1536]{1,0:T(8,128)(2,1)S(1)}, u32[]{:S(2)}, u32[]{:S(2)}) collective-permute-start(bf16[128,1536]{1,0:T(8,128)(2,1)S(1)} %collective-permute-done.10), channel_id=1, source_target_pairs={{0,4},{1,3},{4,8},{5,1},{8,12},{9,5},{12,14},{13,9},{14,10},{15,13... | collective-permute-start | bytes 1179656 | tf_op jit(solution)/shard_map/ppermute | solution.py:49
  22.4 11.8 %collective-permute-start.4 = (bf16[128,1536]{1,0:T(8,128)(2,1)S(1)}, bf16[128,1536]{1,0:T(8,128)(2,1)S(1)}, u32[]{:S(2)}, u32[]{:S(2)}) collective-permute-start(bf16[128,1536]{1,0:T(8,128)(2,1)S(1)} %collective-permute-done.3), channel_id=1, source_target_pairs={{0,4},{1,3},{4,8},{5,1},{8,12},{9,5},{12,14},{13,9},{14,10},{15,13... | collective-permute-start | bytes 1179656 | tf_op jit(solution)/shard_map/ppermute | solution.py:49
  29.0 8.7 %collective-permute-start.16 = (bf16[128,1536]{1,0:T(8,128)(2,1)S(1)}, bf16[128,1536]{1,0:T(8,128)(2,1)S(1)}, u32[]{:S(2)}, u32[]{:S(2)}) collective-permute-start(bf16[128,1536]{1,0:T(8,128)(2,1)S(1)} %convolution_convert_fusion.2), channel_id=1, source_target_pairs={{0,4},{1,3},{4,8},{5,1},{8,12},{9,5},{12,14},{13,9},{14,10},{15,13... | collective-permute-start | bytes 1179656 | tf_op jit(solution)/shard_map/ppermute | solution.py:49
  31.6 9.5 %collective-permute-start.12 = (bf16[128,1536]{1,0:T(8,128)(2,1)S(1)}, bf16[128,1536]{1,0:T(8,128)(2,1)S(1)}, u32[]{:S(2)}, u32[]{:S(2)}) collective-permute-start(bf16[128,1536]{1,0:T(8,128)(2,1)S(1)} %collective-permute-done.11), channel_id=1, source_target_pairs={{0,4},{1,3},{4,8},{5,1},{8,12},{9,5},{12,14},{13,9},{14,10},{15,13... | collective-permute-start | bytes 1179656 | tf_op jit(solution)/shard_map/ppermute | solution.py:49
  34.2 11.1 %collective-permute-start.5 = (bf16[128,1536]{1,0:T(8,128)(2,1)S(1)}, bf16[128,1536]{1,0:T(8,128)(2,1)S(1)}, u32[]{:S(2)}, u32[]{:S(2)}) collective-permute-start(bf16[128,1536]{1,0:T(8,128)(2,1)S(1)} %collective-permute-done.4), channel_id=1, source_target_pairs={{0,4},{1,3},{4,8},{5,1},{8,12},{9,5},{12,14},{13,9},{14,10},{15,13... | collective-permute-start | bytes 1179656 | tf_op jit(solution)/shard_map/ppermute | solution.py:49
  38.2 11.2 %collective-permute-start.17 = (bf16[128,1536]{1,0:T(8,128)(2,1)S(1)}, bf16[128,1536]{1,0:T(8,128)(2,1)S(1)}, u32[]{:S(2)}, u32[]{:S(2)}) collective-permute-start(bf16[128,1536]{1,0:T(8,128)(2,1)S(1)} %fusion.7), channel_id=1, source_target_pairs={{0,4},{1,3},{4,8},{5,1},{8,12},{9,5},{12,14},{13,9},{14,10},{15,13... | collective-permute-start | bytes 1179656 | tf_op jit(solution)/shard_map/ppermute | solution.py:49
  41.0 12.6 %collective-permute-start.13 = (bf16[128,1536]{1,0:T(8,128)(2,1)S(1)}, bf16[128,1536]{1,0:T(8,128)(2,1)S(1)}, u32[]{:S(2)}, u32[]{:S(2)}) collective-permute-start(bf16[128,1536]{1,0:T(8,128)(2,1)S(1)} %collective-permute-done.12), channel_id=1, source_target_pairs={{0,4},{1,3},{4,8},{5,1},{8,12},{9,5},{12,14},{13,9},{14,10},{15,13... | collective-permute-start | bytes 1179656 | tf_op jit(solution)/shard_map/ppermute | solution.py:49
  45.2 12.6 %collective-permute-start.6 = (bf16[128,1536]{1,0:T(8,128)(2,1)S(1)}, bf16[128,1536]{1,0:T(8,128)(2,1)S(1)}, u32[]{:S(2)}, u32[]{:S(2)}) collective-permute-start(bf16[128,1536]{1,0:T(8,128)(2,1)S(1)} %collective-permute-done.5), channel_id=1, source_target_pairs={{0,4},{1,3},{4,8},{5,1},{8,12},{9,5},{12,14},{13,9},{14,10},{15,13... | collective-permute-start | bytes 1179656 | tf_op jit(solution)/shard_map/ppermute | solution.py:49
  49.9 12.2 %collective-permute-start.18 = (bf16[128,1536]{1,0:T(8,128)(2,1)S(1)}, bf16[128,1536]{1,0:T(8,128)(2,1)S(1)}, u32[]{:S(2)}, u32[]{:S(2)}) collective-permute-start(bf16[128,1536]{1,0:T(8,128)(2,1)S(1)} %fusion.6), channel_id=1, source_target_pairs={{0,4},{1,3},{4,8},{5,1},{8,12},{9,5},{12,14},{13,9},{14,10},{15,13... | collective-permute-start | bytes 1179656 | tf_op jit(solution)/shard_map/ppermute | solution.py:49
  53.7 12.6 %collective-permute-start.14 = (bf16[128,1536]{1,0:T(8,128)(2,1)S(1)}, bf16[128,1536]{1,0:T(8,128)(2,1)S(1)}, u32[]{:S(2)}, u32[]{:S(2)}) collective-permute-start(bf16[128,1536]{1,0:T(8,128)(2,1)S(1)} %collective-permute-done.13), channel_id=1, source_target_pairs={{0,4},{1,3},{4,8},{5,1},{8,12},{9,5},{12,14},{13,9},{14,10},{15,13... | collective-permute-start | bytes 1179656 | tf_op jit(solution)/shard_map/ppermute | solution.py:49
  57.9 12.6 %collective-permute-start.7 = (bf16[128,1536]{1,0:T(8,128)(2,1)S(1)}, bf16[128,1536]{1,0:T(8,128)(2,1)S(1)}, u32[]{:S(2)}, u32[]{:S(2)}) collective-permute-start(bf16[128,1536]{1,0:T(8,128)(2,1)S(1)} %collective-permute-done.6), channel_id=1, source_target_pairs={{0,4},{1,3},{4,8},{5,1},{8,12},{9,5},{12,14},{13,9},{14,10},{15,13... | collective-permute-start | bytes 1179656 | tf_op jit(solution)/shard_map/ppermute | solution.py:49
  62.6 22.1 %collective-permute-start.19 = (bf16[128,1536]{1,0:T(8,128)(2,1)S(1)}, bf16[128,1536]{1,0:T(8,128)(2,1)S(1)}, u32[]{:S(2)}, u32[]{:S(2)}) collective-permute-start(bf16[128,1536]{1,0:T(8,128)(2,1)S(1)} %fusion.5), channel_id=1, source_target_pairs={{0,4},{1,3},{4,8},{5,1},{8,12},{9,5},{12,14},{13,9},{14,10},{15,13... | collective-permute-start | bytes 1179656 | tf_op jit(solution)/shard_map/ppermute | solution.py:49
  66.3 12.6 %collective-permute-start.15 = (bf16[128,1536]{1,0:T(8,128)(2,1)S(1)}, bf16[128,1536]{1,0:T(8,128)(2,1)S(1)}, u32[]{:S(2)}, u32[]{:S(2)}) collective-permute-start(bf16[128,1536]{1,0:T(8,128)(2,1)S(1)} %collective-permute-done.14), channel_id=1, source_target_pairs={{0,4},{1,3},{4,8},{5,1},{8,12},{9,5},{12,14},{13,9},{14,10},{15,13... | collective-permute-start | bytes 1179656 | tf_op jit(solution)/shard_map/ppermute | solution.py:49
  70.5 12.6 %collective-permute-start.8 = (bf16[128,1536]{1,0:T(8,128)(2,1)S(1)}, bf16[128,1536]{1,0:T(8,128)(2,1)S(1)}, u32[]{:S(2)}, u32[]{:S(2)}) collective-permute-start(bf16[128,1536]{1,0:T(8,128)(2,1)S(1)} %collective-permute-done.7), channel_id=1, source_target_pairs={{0,4},{1,3},{4,8},{5,1},{8,12},{9,5},{12,14},{13,9},{14,10},{15,13... | collective-permute-start | bytes 1179656 | tf_op jit(solution)/shard_map/ppermute | solution.py:49
  84.6 18.8 %collective-permute-start.24 = (bf16[384,1536]{1,0:T(8,128)(2,1)S(1)}, bf16[384,1536]{1,0:T(8,128)(2,1)S(1)}, u32[]{:S(2)}, u32[]{:S(2)}) collective-permute-start(bf16[384,1536]{1,0:T(8,128)(2,1)S(1)} %convolution_convert_fusion), channel_id=1, source_target_pairs={{0,1},{1,0},{2,3},{3,2},{4,5},{5,4},{6,7},{7,6},{8,9},{9,8},{10,11... | collective-permute-start | bytes 3538952 | tf_op jit(solution)/shard_map/ppermute | solution.py:52
  85.2 7.8 %collective-permute-start.20 = (bf16[128,1536]{1,0:T(8,128)(2,1)S(1)}, bf16[128,1536]{1,0:T(8,128)(2,1)S(1)}, u32[]{:S(2)}, u32[]{:S(2)}) collective-permute-start(bf16[128,1536]{1,0:T(8,128)(2,1)S(1)} %fusion.4), channel_id=1, source_target_pairs={{0,4},{1,3},{4,8},{5,1},{8,12},{9,5},{12,14},{13,9},{14,10},{15,13... | collective-permute-start | bytes 1179656 | tf_op jit(solution)/shard_map/ppermute | solution.py:49
  89.2 17.1 %collective-permute-start.23 = (bf16[384,1536]{1,0:T(8,128)(2,1)S(1)}, bf16[384,1536]{1,0:T(8,128)(2,1)S(1)}, u32[]{:S(2)}, u32[]{:S(2)}) collective-permute-start(bf16[384,1536]{1,0:T(8,128)(2,1)S(1)} %convolution_convert_fusion.1), channel_id=1, source_target_pairs={{0,1},{1,0},{2,3},{3,2},{4,5},{5,4},{6,7},{7,6},{8,9},{9,8},{10,11... | collective-permute-start | bytes 3538952 | tf_op jit(solution)/shard_map/ppermute | solution.py:52
  93.5 7.8 %collective-permute-start.21 = (bf16[128,1536]{1,0:T(8,128)(2,1)S(1)}, bf16[128,1536]{1,0:T(8,128)(2,1)S(1)}, u32[]{:S(2)}, u32[]{:S(2)}) collective-permute-start(bf16[128,1536]{1,0:T(8,128)(2,1)S(1)} %fusion.3), channel_id=1, source_target_pairs={{0,4},{1,3},{4,8},{5,1},{8,12},{9,5},{12,14},{13,9},{14,10},{15,13... | collective-permute-start | bytes 1179656 | tf_op jit(solution)/shard_map/ppermute | solution.py:49
  101.8 7.8 %collective-permute-start.22 = (bf16[128,1536]{1,0:T(8,128)(2,1)S(1)}, bf16[128,1536]{1,0:T(8,128)(2,1)S(1)}, u32[]{:S(2)}, u32[]{:S(2)}) collective-permute-start(bf16[128,1536]{1,0:T(8,128)(2,1)S(1)} %fusion.2), channel_id=1, source_target_pairs={{0,4},{1,3},{4,8},{5,1},{8,12},{9,5},{12,14},{13,9},{14,10},{15,13... | collective-permute-start | bytes 1179656 | tf_op jit(solution)/shard_map/ppermute | solution.py:49

commit v2 on v1

v2 whole, which is shorter than its diff:
```python
import jax
import jax.numpy as jnp
from jax import lax
from jax.sharding import PartitionSpec as P

LEVELS = 16
LAST = (((1,), (1,)), ((), ()))
ROWS = (((1,), (0,)), ((), ()))
FIRST = (((0,), (0,)), ((), ()))


def ring_order(chips):
    if chips <= 8:
        return list(range(0, chips, 2)) + list(range(1, chips, 2))[::-1]
    return list(range(chips))


def ring_route(count):
    order = ring_order(count // 2)
    chips = len(order)
    route = []
    for place in range(chips):
        here = order[place]
        route.append((2 * here, 2 * order[(place + 1) % chips]))
        route.append((2 * here + 1, 2 * order[(place - 1) % chips] + 1))
    return route


def gelu_pair(v):
    inner = 0.7978845608 * (v + 0.044715 * v * v * v)
    hyper = jnp.tanh(inner)
    value = 0.5 * v * (1.0 + hyper)
    slope = 0.5 * (1.0 + hyper) + 0.5 * v * (1.0 - hyper * hyper) * 0.7978845608 * (
        1.0 + 3.0 * 0.044715 * v * v
    )
    return value, slope


def dot(a, b, dims):
    return lax.dot_general(a, b, dims, preferred_element_type=jnp.float32)


def behind(block, *earlier):
    return lax.optimization_barrier((block, earlier))[0]


def local(tokens, upstream, sample_of_token, reward_level, up_weight, down_weight):
    count = lax.axis_size("gx")
    chips = count // 2
    route = ring_route(count)
    swap = [(i, i ^ 1) for i in range(count)]

    def hop(block, name):
        with jax.named_scope(name):
            return lax.ppermute(block, "gx", route)

    def across(block, name):
        with jax.named_scope(name):
            return lax.ppermute(block, "gx", swap)

    x_next = hop(tokens, "hop_x")
    matches = sample_of_token[:, None] == jnp.arange(reward_level.shape[0], dtype=jnp.int32)[None, :]
    level = jnp.sum(jnp.where(matches, reward_level[None, :], 0), axis=1)
    weight = (level + 1).astype(jnp.float32) / LEVELS
    weighted = (weight[:, None] * behind(upstream, tokens, up_weight).astype(jnp.float32)).astype(jnp.bfloat16)
    g_next = hop(weighted, "hop_g")


    units = up_weight.shape[0]
    own, other = slice(0, units), slice(units, None)
    up_rows = jnp.concatenate([up_weight, across(up_weight, "swap_up")], axis=0)
    down_rows = jnp.concatenate([down_weight, across(down_weight, "swap_down")], axis=0)

    def middle(x, g):
        value, slope = gelu_pair(dot(x, up_rows, LAST))
        hidden = value.astype(jnp.bfloat16)
        return x, g, hidden, (dot(g, down_rows, LAST) * slope).astype(jnp.bfloat16)

    def gradients(waiting, side):
        x, g, hidden, grad_pre = [jnp.concatenate(blocks) for blocks in zip(*waiting)]
        return [dot(grad_pre[:, side], x, FIRST), dot(hidden[:, side], g, FIRST)]

    def add(sums, more):
        return more if sums is None else [a + b for a, b in zip(sums, more)]

    due = []
    waiting, mine, theirs, carried, base = [], None, None, None, None
    for step in range(1, chips):
        x, g = x_next, g_next
        if step == 1:
            g = behind(g, dot(x, up_rows, LAST))
        if step < chips - 1:
            x_next, g_next = hop(x, "hop_x"), hop(g, "hop_g")
        waiting.append(middle(x, g))
        if step == chips - 1:
            with jax.named_scope("last"):
                mine = add(mine, gradients(waiting, own))
                theirs = [a.astype(jnp.bfloat16) for a in add(theirs, gradients(waiting, other))]
            carried = behind(carried, waiting[-1], theirs)
        with jax.named_scope("token_part"):
            total = dot(waiting[-1][3], up_rows, ROWS)
            if carried is not None:
                total = total + carried.astype(jnp.float32)
            total = total.astype(jnp.bfloat16)
        arrived = carried
        carried = hop(total, "hop_sum")
        done = [total]
        if step == 1:
            waiting.append(middle(behind(tokens, total), weighted))
            base = weighted.astype(jnp.float32) + dot(waiting[-1][3], up_rows, ROWS)
        elif step == 2:
            done.append(base)
        done += due
        if step in (chips // 2, chips - 3):
            with jax.named_scope("batch"):
                waiting = [behind(blocks, total) for blocks in waiting]
                mine = add(mine, gradients(waiting, own))
                theirs = add(theirs, gradients(waiting, other))
            waiting = []
            due = mine + theirs
        if step < chips - 1:
            x_next, g_next = behind(x_next, *done), behind(g_next, *done)

    received = [across(behind(a, arrived), "swap_grads") for a in theirs]
    with jax.named_scope("finish"):
        grad_up, grad_down = [a + b.astype(jnp.float32) for a, b in zip(mine, received)]
        carried, grad_up, grad_down = lax.optimization_barrier((carried, grad_up, grad_down))
        grad_tokens = (base + carried.astype(jnp.float32)).astype(jnp.bfloat16)
    return grad_tokens, grad_up, grad_down


def solution(mesh):
    rows = P(("groups", "gx"), None)
    return jax.shard_map(
        local,
        mesh=mesh,
        in_specs=(rows, rows, P(("groups", "gx")), P("groups"), P("gx", None), P("gx", None)),
        out_specs=(rows, rows, rows),
        check_vma=False,
    )
```

time: 111 us -> 100 us (0.901)
  waiting for transfers between devices: 41.4 us -> 21.1 us
  starting transfers between devices: 36.4 us -> 42.7 us
  matrix products: 28.2 us -> 30.1 us
    ppermute x21, waiting for transfers between devices: 41.4 us -> 21.1 us  [hop(): return lax.ppermute(block, 'gx', route)]
    ppermute x21, starting transfers between devices: 35.7 us -> 41.6 us  [hop(): return lax.ppermute(block, 'gx', route)]
    convert_element_type x0 -> x2, other arithmetic: none -> 1.94 us  [the longest x1 1.13 us: local(): (weight[:, None] * behind(upstream, tokens, up_weight).astype(jnp.float32...]
    dot_general x28 -> x36, matrix products: 28.2 us -> 30.1 us  [dot(): return lax.dot_general(a, b, dims, preferred_element_type=jnp.float32)]
    unnamed x1 -> x0, other arithmetic: 1.13 us -> none
  transfers between devices with their start and end apart: 25 -> 25, of which waited for: 17 -> 14; matrix products, arithmetic and copies ran while one was open for 28% -> 34% of each run, Pallas kernels for 0% -> 0%
where the time goes in v2:
time: 100 us; the launch traced here: 99.8 us
  starting transfers between devices  42.7 us (43%)
  matrix products  30.1 us (30%)
  waiting for transfers between devices  21.1 us (21%)
  other arithmetic  2.71 us (3%)
  local copies, waits for them, and re-layouts  2.12 us (2%)
  between operations  1.11 us (1%)
    ppermute x21, starting transfers between devices, hop(): return lax.ppermute(block, 'gx', route)  41.6 us
    dot_general x36, matrix products, dot(): return lax.dot_general(a, b, dims, preferred_element_type=jnp.float32)  30.1 us
    ppermute x21, waiting for transfers between devices, hop(): return lax.ppermute(block, 'gx', route)  21.1 us
  transfers between devices with their start and end apart: 25, of which 14 were waited for; matrix products, arithmetic and copies ran while one was open for 34% of the time, Pallas kernels for 0%

profile of v2, /device:TPU:0, one launch (start us, length us, event | category | flops | bytes accessed | tf_op | source)
XLA Modules:
  0.0 99.8 jit_solution(13839789067696878708)
XLA Ops:
  1.2 3.0 %collective-permute-start.3 = (bf16[128,1536]{1,0:T(8,128)(2,1)}, bf16[128,1536]{1,0:T(8,128)(2,1)S(1)}, u32[]{:S(2)}, u32[]{:S(2)}) collective-permute-start(bf16[128,1536]{1,0:T(8,128)(2,1)} %param.6), channel_id=1, source_target_pairs={{0,4},{1,3},{4,8},{5,1},{8,12},{9,5},{12,14},{13,9},{14,10},{15,13... | collective-permute-start | bytes 1179656 | tf_op jit(solution)/shard_map/hop_x/ppermute | solution.py:55
  6.1 1.6 %collective-permute-start.1 = (bf16[128,1536]{1,0:T(8,128)(2,1)S(1)}, bf16[128,1536]{1,0:T(8,128)(2,1)S(1)}, u32[]{:S(2)}, u32[]{:S(2)}) collective-permute-start(bf16[128,1536]{1,0:T(8,128)(2,1)S(1)} %multiply_convert_fusion), channel_id=1, source_target_pairs={{0,4},{1,3},{4,8},{5,1},{8,12},{9,5},{12,14},{13,9},{14,10},{15,13... | collective-permute-start | bytes 1179656 | tf_op jit(solution)/shard_map/hop_g/ppermute | solution.py:55
  7.8 1.3 %constant_dynamic-update-slice_fusion.1 = bf16[768,1536]{1,0:T(8,128)(2,1)S(1)} fusion(bf16[384,1536]{1,0:T(8,128)(2,1)} %param.11), kind=kLoop, calls=%fused_computation.132 | loop fusion | bytes 2359296
  10.1 2.1 %collective-permute-start.6 = (bf16[128,1536]{1,0:T(8,128)(2,1)S(1)}, bf16[128,1536]{1,0:T(8,128)(2,1)S(1)}, u32[]{:S(2)}, u32[]{:S(2)}) collective-permute-start(bf16[128,1536]{1,0:T(8,128)(2,1)S(1)} %collective-permute-done.3), channel_id=1, source_target_pairs={{0,4},{1,3},{4,8},{5,1},{8,12},{9,5},{12,14},{13,9},{14,10},{15,13... | collective-permute-start | bytes 1179656 | tf_op jit(solution)/shard_map/hop_x/ppermute | solution.py:55
  14.4 2.1 %collective-permute-start.4 = (bf16[128,1536]{1,0:T(8,128)(2,1)S(1)}, bf16[128,1536]{1,0:T(8,128)(2,1)S(1)}, u32[]{:S(2)}, u32[]{:S(2)}) collective-permute-start(bf16[128,1536]{1,0:T(8,128)(2,1)S(1)} %collective-permute-done.1), channel_id=1, source_target_pairs={{0,4},{1,3},{4,8},{5,1},{8,12},{9,5},{12,14},{13,9},{14,10},{15,13... | collective-permute-start | bytes 1179656 | tf_op jit(solution)/shard_map/hop_g/ppermute | solution.py:55
  18.0 1.6 %collective-permute-start.7 = (bf16[128,1536]{1,0:T(8,128)(2,1)S(1)}, bf16[128,1536]{1,0:T(8,128)(2,1)S(1)}, u32[]{:S(2)}, u32[]{:S(2)}) collective-permute-start(bf16[128,1536]{1,0:T(8,128)(2,1)S(1)} %convolution_convert_fusion), channel_id=1, source_target_pairs={{0,4},{1,3},{4,8},{5,1},{8,12},{9,5},{12,14},{13,9},{14,10},{15,13... | collective-permute-start | bytes 1179656 | tf_op jit(solution)/shard_map/hop_sum/ppermute | solution.py:55
  20.6 1.6 %collective-permute-start.9 = (bf16[128,1536]{1,0:T(8,128)(2,1)S(1)}, bf16[128,1536]{1,0:T(8,128)(2,1)S(1)}, u32[]{:S(2)}, u32[]{:S(2)}) collective-permute-start(bf16[128,1536]{1,0:T(8,128)(2,1)S(1)} %collective-permute-done.6), channel_id=1, source_target_pairs={{0,4},{1,3},{4,8},{5,1},{8,12},{9,5},{12,14},{13,9},{14,10},{15,13... | collective-permute-start | bytes 1179656 | tf_op jit(solution)/shard_map/hop_x/ppermute | solution.py:55
  24.6 1.6 %collective-permute-start.5 = (bf16[128,1536]{1,0:T(8,128)(2,1)S(1)}, bf16[128,1536]{1,0:T(8,128)(2,1)S(1)}, u32[]{:S(2)}, u32[]{:S(2)}) collective-permute-start(bf16[128,1536]{1,0:T(8,128)(2,1)S(1)} %collective-permute-done.4), channel_id=1, source_target_pairs={{0,4},{1,3},{4,8},{5,1},{8,12},{9,5},{12,14},{13,9},{14,10},{15,13... | collective-permute-start | bytes 1179656 | tf_op jit(solution)/shard_map/hop_g/ppermute | solution.py:55
  27.6 2.0 %collective-permute-start.10 = (bf16[128,1536]{1,0:T(8,128)(2,1)S(1)}, bf16[128,1536]{1,0:T(8,128)(2,1)S(1)}, u32[]{:S(2)}, u32[]{:S(2)}) collective-permute-start(bf16[128,1536]{1,0:T(8,128)(2,1)S(1)} %fusion.4), channel_id=1, source_target_pairs={{0,4},{1,3},{4,8},{5,1},{8,12},{9,5},{12,14},{13,9},{14,10},{15,13... | collective-permute-start | bytes 1179656 | tf_op jit(solution)/shard_map/hop_sum/ppermute | solution.py:55
  29.6 1.6 %collective-permute-done.9 = bf16[128,1536]{1,0:T(8,128)(2,1)S(1)} collective-permute-done((bf16[128,1536]{1,0:T(8,128)(2,1)S(1)}, bf16[128,1536]{1,0:T(8,128)(2,1)S(1)}, u32[]{:S(2)}, u32[]{:S(2)}) %collective-permute-start.9) | collective-permute-done | bytes 393248 | tf_op jit(solution)/shard_map/hop_x/ppermute | solution.py:55
  32.2 2.1 %collective-permute-start.12 = (bf16[128,1536]{1,0:T(8,128)(2,1)S(1)}, bf16[128,1536]{1,0:T(8,128)(2,1)S(1)}, u32[]{:S(2)}, u32[]{:S(2)}) collective-permute-start(bf16[128,1536]{1,0:T(8,128)(2,1)S(1)} %collective-permute-done.9), channel_id=1, source_target_pairs={{0,4},{1,3},{4,8},{5,1},{8,12},{9,5},{12,14},{13,9},{14,10},{15,13... | collective-permute-start | bytes 1179656 | tf_op jit(solution)/shard_map/hop_x/ppermute | solution.py:55
  35.4 2.1 %collective-permute-start.8 = (bf16[128,1536]{1,0:T(8,128)(2,1)S(1)}, bf16[128,1536]{1,0:T(8,128)(2,1)S(1)}, u32[]{:S(2)}, u32[]{:S(2)}) collective-permute-start(bf16[128,1536]{1,0:T(8,128)(2,1)S(1)} %collective-permute-done.5), channel_id=1, source_target_pairs={{0,4},{1,3},{4,8},{5,1},{8,12},{9,5},{12,14},{13,9},{14,10},{15,13... | collective-permute-start | bytes 1179656 | tf_op jit(solution)/shard_map/hop_g/ppermute | solution.py:55
  38.5 1.2 %collective-permute-done.10 = bf16[128,1536]{1,0:T(8,128)(2,1)S(1)} collective-permute-done((bf16[128,1536]{1,0:T(8,128)(2,1)S(1)}, bf16[128,1536]{1,0:T(8,128)(2,1)S(1)}, u32[]{:S(2)}, u32[]{:S(2)}) %collective-permute-start.10) | collective-permute-done | bytes 393248 | tf_op jit(solution)/shard_map/hop_sum/ppermute | solution.py:55
  40.1 2.1 %collective-permute-start.13 = (bf16[128,1536]{1,0:T(8,128)(2,1)S(1)}, bf16[128,1536]{1,0:T(8,128)(2,1)S(1)}, u32[]{:S(2)}, u32[]{:S(2)}) collective-permute-start(bf16[128,1536]{1,0:T(8,128)(2,1)S(1)} %fusion.5), channel_id=1, source_target_pairs={{0,4},{1,3},{4,8},{5,1},{8,12},{9,5},{12,14},{13,9},{14,10},{15,13... | collective-permute-start | bytes 1179656 | tf_op jit(solution)/shard_map/hop_sum/ppermute | solution.py:55
  42.3 1.6 %collective-permute-done.12 = bf16[128,1536]{1,0:T(8,128)(2,1)S(1)} collective-permute-done((bf16[128,1536]{1,0:T(8,128)(2,1)S(1)}, bf16[128,1536]{1,0:T(8,128)(2,1)S(1)}, u32[]{:S(2)}, u32[]{:S(2)}) %collective-permute-start.12) | collective-permute-done | bytes 393248 | tf_op jit(solution)/shard_map/hop_x/ppermute | solution.py:55
  44.8 2.1 %collective-permute-start.15 = (bf16[128,1536]{1,0:T(8,128)(2,1)S(1)}, bf16[128,1536]{1,0:T(8,128)(2,1)S(1)}, u32[]{:S(2)}, u32[]{:S(2)}) collective-permute-start(bf16[128,1536]{1,0:T(8,128)(2,1)S(1)} %collective-permute-done.12), channel_id=1, source_target_pairs={{0,4},{1,3},{4,8},{5,1},{8,12},{9,5},{12,14},{13,9},{14,10},{15,13... | collective-permute-start | bytes 1179656 | tf_op jit(solution)/shard_map/hop_x/ppermute | solution.py:55
  48.1 2.1 %collective-permute-start.11 = (bf16[128,1536]{1,0:T(8,128)(2,1)S(1)}, bf16[128,1536]{1,0:T(8,128)(2,1)S(1)}, u32[]{:S(2)}, u32[]{:S(2)}) collective-permute-start(bf16[128,1536]{1,0:T(8,128)(2,1)S(1)} %collective-permute-done.8), channel_id=1, source_target_pairs={{0,4},{1,3},{4,8},{5,1},{8,12},{9,5},{12,14},{13,9},{14,10},{15,13... | collective-permute-start | bytes 1179656 | tf_op jit(solution)/shard_map/hop_g/ppermute | solution.py:55
  51.1 1.2 %collective-permute-done.13 = bf16[128,1536]{1,0:T(8,128)(2,1)S(1)} collective-permute-done((bf16[128,1536]{1,0:T(8,128)(2,1)S(1)}, bf16[128,1536]{1,0:T(8,128)(2,1)S(1)}, u32[]{:S(2)}, u32[]{:S(2)}) %collective-permute-start.13) | collective-permute-done | bytes 393248 | tf_op jit(solution)/shard_map/hop_sum/ppermute | solution.py:55
  52.8 2.3 %collective-permute-start.16 = (bf16[128,1536]{1,0:T(8,128)(2,1)S(1)}, bf16[128,1536]{1,0:T(8,128)(2,1)S(1)}, u32[]{:S(2)}, u32[]{:S(2)}) collective-permute-start(bf16[128,1536]{1,0:T(8,128)(2,1)S(1)} %fusion.6), channel_id=1, source_target_pairs={{0,4},{1,3},{4,8},{5,1},{8,12},{9,5},{12,14},{13,9},{14,10},{15,13... | collective-permute-start | bytes 1179656 | tf_op jit(solution)/shard_map/hop_sum/ppermute | solution.py:55
  61.0 1.6 %collective-permute-start.18 = (bf16[128,1536]{1,0:T(8,128)(2,1)S(1)}, bf16[128,1536]{1,0:T(8,128)(2,1)S(1)}, u32[]{:S(2)}, u32[]{:S(2)}) collective-permute-start(bf16[128,1536]{1,0:T(8,128)(2,1)S(1)} %collective-permute-done.15), channel_id=1, source_target_pairs={{0,4},{1,3},{4,8},{5,1},{8,12},{9,5},{12,14},{13,9},{14,10},{15,13... | collective-permute-start | bytes 1179656 | tf_op jit(solution)/shard_map/hop_x/ppermute | solution.py:55
  62.7 1.6 %collective-permute-start.14 = (bf16[128,1536]{1,0:T(8,128)(2,1)S(1)}, bf16[128,1536]{1,0:T(8,128)(2,1)S(1)}, u32[]{:S(2)}, u32[]{:S(2)}) collective-permute-start(bf16[128,1536]{1,0:T(8,128)(2,1)S(1)} %collective-permute-done.11), channel_id=1, source_target_pairs={{0,4},{1,3},{4,8},{5,1},{8,12},{9,5},{12,14},{13,9},{14,10},{15,13... | collective-permute-start | bytes 1179656 | tf_op jit(solution)/shard_map/hop_g/ppermute | solution.py:55
  65.7 1.9 %collective-permute-start.19 = (bf16[128,1536]{1,0:T(8,128)(2,1)S(1)}, bf16[128,1536]{1,0:T(8,128)(2,1)S(1)}, u32[]{:S(2)}, u32[]{:S(2)}) collective-permute-start(bf16[128,1536]{1,0:T(8,128)(2,1)S(1)} %fusion.7), channel_id=1, source_target_pairs={{0,4},{1,3},{4,8},{5,1},{8,12},{9,5},{12,14},{13,9},{14,10},{15,13... | collective-permute-start | bytes 1179656 | tf_op jit(solution)/shard_map/hop_sum/ppermute | solution.py:55
  69.5 1.7 %collective-permute-start.20 = (bf16[128,1536]{1,0:T(8,128)(2,1)S(1)}, bf16[128,1536]{1,0:T(8,128)(2,1)S(1)}, u32[]{:S(2)}, u32[]{:S(2)}) collective-permute-start(bf16[128,1536]{1,0:T(8,128)(2,1)S(1)} %collective-permute-done.18), channel_id=1, source_target_pairs={{0,4},{1,3},{4,8},{5,1},{8,12},{9,5},{12,14},{13,9},{14,10},{15,13... | collective-permute-start | bytes 1179656 | tf_op jit(solution)/shard_map/hop_x/ppermute | solution.py:55
  73.3 2.1 %collective-permute-start.17 = (bf16[128,1536]{1,0:T(8,128)(2,1)S(1)}, bf16[128,1536]{1,0:T(8,128)(2,1)S(1)}, u32[]{:S(2)}, u32[]{:S(2)}) collective-permute-start(bf16[128,1536]{1,0:T(8,128)(2,1)S(1)} %collective-permute-done.14), channel_id=1, source_target_pairs={{0,4},{1,3},{4,8},{5,1},{8,12},{9,5},{12,14},{13,9},{14,10},{15,13... | collective-permute-start | bytes 1179656 | tf_op jit(solution)/shard_map/hop_g/ppermute | solution.py:55
  78.0 2.1 %collective-permute-start.21 = (bf16[128,1536]{1,0:T(8,128)(2,1)S(1)}, bf16[128,1536]{1,0:T(8,128)(2,1)S(1)}, u32[]{:S(2)}, u32[]{:S(2)}) collective-permute-start(bf16[128,1536]{1,0:T(8,128)(2,1)S(1)} %fusion.8), channel_id=1, source_target_pairs={{0,4},{1,3},{4,8},{5,1},{8,12},{9,5},{12,14},{13,9},{14,10},{15,13... | collective-permute-start | bytes 1179656 | tf_op jit(solution)/shard_map/hop_sum/ppermute | solution.py:55
  80.2 1.6 %collective-permute-done.20 = bf16[128,1536]{1,0:T(8,128)(2,1)S(1)} collective-permute-done((bf16[128,1536]{1,0:T(8,128)(2,1)S(1)}, bf16[128,1536]{1,0:T(8,128)(2,1)S(1)}, u32[]{:S(2)}, u32[]{:S(2)}) %collective-permute-start.20) | collective-permute-done | bytes 393248 | tf_op jit(solution)/shard_map/hop_x/ppermute | solution.py:55
  82.8 3.2 %collective-permute-done.17 = bf16[128,1536]{1,0:T(8,128)(2,1)S(1)} collective-permute-done((bf16[128,1536]{1,0:T(8,128)(2,1)S(1)}, bf16[128,1536]{1,0:T(8,128)(2,1)S(1)}, u32[]{:S(2)}, u32[]{:S(2)}) %collective-permute-start.17) | collective-permute-done | bytes 393248 | tf_op jit(solution)/shard_map/hop_g/ppermute | solution.py:55
  88.0 2.2 %collective-permute-done.21 = bf16[128,1536]{1,0:T(8,128)(2,1)S(1)} collective-permute-done((bf16[128,1536]{1,0:T(8,128)(2,1)S(1)}, bf16[128,1536]{1,0:T(8,128)(2,1)S(1)}, u32[]{:S(2)}, u32[]{:S(2)}) %collective-permute-start.21) | collective-permute-done | bytes 393248 | tf_op jit(solution)/shard_map/hop_sum/ppermute | solution.py:55
  91.2 2.1 %collective-permute-start.22 = (bf16[128,1536]{1,0:T(8,128)(2,1)S(1)}, bf16[128,1536]{1,0:T(8,128)(2,1)S(1)}, u32[]{:S(2)}, u32[]{:S(2)}) collective-permute-start(bf16[128,1536]{1,0:T(8,128)(2,1)S(1)} %fusion.9), channel_id=1, source_target_pairs={{0,4},{1,3},{4,8},{5,1},{8,12},{9,5},{12,14},{13,9},{14,10},{15,13... | collective-permute-start | bytes 1179656 | tf_op jit(solution)/shard_map/hop_sum/ppermute | solution.py:55
  93.3 1.9 %fusion.1 = f32[384,1536]{1,0:T(8,128)} fusion(f32[384,1536]{1,0:T(8,128)S(1)} %convolution_add_fusion.7, bf16[256,1536]{1,0:T(8,128)(2,1)S(1)} %constant_dynamic-update-slice_fusion.24, bf16[384,1536]{1,0:T(8,128)(2,1)S(1)} %collective-permute-done.23, bf16[128,768]{1,0:T(8,128)(2,1)S(1)} %fusion.17, bf16[128,768]{1,0:T(8,128)(2,1)S(1)} %fusion.16), kind=kOutput, calls=%fused_computation.3 | convolution fusion | flops 304152576 | bytes 7077888 | tf_op jit(solution)/shard_map/last/dot_general | solution.py:40
  95.2 1.9 %fusion = f32[384,1536]{1,0:T(8,128)} fusion(f32[384,1536]{1,0:T(8,128)S(1)} %convolution_add_fusion.6, bf16[256,1536]{1,0:T(8,128)(2,1)S(1)} %constant_dynamic-update-slice_fusion.26, bf16[384,1536]{1,0:T(8,128)(2,1)S(1)} %collective-permute-done.24, bf16[128,768]{1,0:T(8,128)(2,1)S(1)} %get-tuple-element.105, bf16[128,768]{1,0:T(8,128)(2,1)S(1)} %get-tuple-element.107), kind=kOutput, calls=%fused_computation.1 | convolution fusion | flops 304152576 | bytes 7077888 | tf_op jit(solution)/shard_map/last/dot_general | solution.py:40
  97.1 1.9 %collective-permute-done.22 = bf16[128,1536]{1,0:T(8,128)(2,1)S(1)} collective-permute-done((bf16[128,1536]{1,0:T(8,128)(2,1)S(1)}, bf16[128,1536]{1,0:T(8,128)(2,1)S(1)}, u32[]{:S(2)}, u32[]{:S(2)}) %collective-permute-start.22) | collective-permute-done | bytes 393248 | tf_op jit(solution)/shard_map/hop_sum/ppermute | solution.py:55
  (88 shorter events, 37.5 us)
Async XLA Ops:
  0.6 8.5 %copy-start.1 = (bf16[384,1536]{1,0:T(8,128)(2,1)S(1)}, bf16[384,1536]{1,0:T(8,128)(2,1)}, u32[]{:S(2)}) copy-start(bf16[384,1536]{1,0:T(8,128)(2,1)} %param.10) | copy-start | bytes 3538948
  0.6 15.8 %collective-permute-start = (bf16[384,1536]{1,0:T(8,128)(2,1)}, bf16[384,1536]{1,0:T(8,128)(2,1)S(1)}, u32[]{:S(2)}, u32[]{:S(2)}) collective-permute-start(bf16[384,1536]{1,0:T(8,128)(2,1)} %param.11), channel_id=1, source_target_pairs={{0,1},{1,0},{2,3},{3,2},{4,5},{5,4},{6,7},{7,6},{8,9},{9,8},{10,11... | collective-permute-start | bytes 3538952 | tf_op jit(solution)/shard_map/swap_down/ppermute | solution.py:59
  1.2 11.1 %collective-permute-start.2 = (bf16[384,1536]{1,0:T(8,128)(2,1)}, bf16[384,1536]{1,0:T(8,128)(2,1)S(1)}, u32[]{:S(2)}, u32[]{:S(2)}) collective-permute-start(bf16[384,1536]{1,0:T(8,128)(2,1)} %param.10), channel_id=1, source_target_pairs={{0,1},{1,0},{2,3},{3,2},{4,5},{5,4},{6,7},{7,6},{8,9},{9,8},{10,11... | collective-permute-start | bytes 3538952 | tf_op jit(solution)/shard_map/swap_up/ppermute | solution.py:59
  1.2 8.9 %collective-permute-start.3 = (bf16[128,1536]{1,0:T(8,128)(2,1)}, bf16[128,1536]{1,0:T(8,128)(2,1)S(1)}, u32[]{:S(2)}, u32[]{:S(2)}) collective-permute-start(bf16[128,1536]{1,0:T(8,128)(2,1)} %param.6), channel_id=1, source_target_pairs={{0,4},{1,3},{4,8},{5,1},{8,12},{9,5},{12,14},{13,9},{14,10},{15,13... | collective-permute-start | bytes 1179656 | tf_op jit(solution)/shard_map/hop_x/ppermute | solution.py:55
  6.1 8.2 %collective-permute-start.1 = (bf16[128,1536]{1,0:T(8,128)(2,1)S(1)}, bf16[128,1536]{1,0:T(8,128)(2,1)S(1)}, u32[]{:S(2)}, u32[]{:S(2)}) collective-permute-start(bf16[128,1536]{1,0:T(8,128)(2,1)S(1)} %multiply_convert_fusion), channel_id=1, source_target_pairs={{0,4},{1,3},{4,8},{5,1},{8,12},{9,5},{12,14},{13,9},{14,10},{15,13... | collective-permute-start | bytes 1179656 | tf_op jit(solution)/shard_map/hop_g/ppermute | solution.py:55
  10.1 9.5 %collective-permute-start.6 = (bf16[128,1536]{1,0:T(8,128)(2,1)S(1)}, bf16[128,1536]{1,0:T(8,128)(2,1)S(1)}, u32[]{:S(2)}, u32[]{:S(2)}) collective-permute-start(bf16[128,1536]{1,0:T(8,128)(2,1)S(1)} %collective-permute-done.3), channel_id=1, source_target_pairs={{0,4},{1,3},{4,8},{5,1},{8,12},{9,5},{12,14},{13,9},{14,10},{15,13... | collective-permute-start | bytes 1179656 | tf_op jit(solution)/shard_map/hop_x/ppermute | solution.py:55
  14.4 10.2 %collective-permute-start.4 = (bf16[128,1536]{1,0:T(8,128)(2,1)S(1)}, bf16[128,1536]{1,0:T(8,128)(2,1)S(1)}, u32[]{:S(2)}, u32[]{:S(2)}) collective-permute-start(bf16[128,1536]{1,0:T(8,128)(2,1)S(1)} %collective-permute-done.1), channel_id=1, source_target_pairs={{0,4},{1,3},{4,8},{5,1},{8,12},{9,5},{12,14},{13,9},{14,10},{15,13... | collective-permute-start | bytes 1179656 | tf_op jit(solution)/shard_map/hop_g/ppermute | solution.py:55
  18.0 4.2 %copy-start = (bf16[128,1536]{1,0:T(8,128)(2,1)S(1)}, bf16[128,1536]{1,0:T(8,128)(2,1)}, u32[]{:S(2)}) copy-start(bf16[128,1536]{1,0:T(8,128)(2,1)} %param.6) | copy-start | bytes 1179652
  18.0 9.1 %collective-permute-start.7 = (bf16[128,1536]{1,0:T(8,128)(2,1)S(1)}, bf16[128,1536]{1,0:T(8,128)(2,1)S(1)}, u32[]{:S(2)}, u32[]{:S(2)}) collective-permute-start(bf16[128,1536]{1,0:T(8,128)(2,1)S(1)} %convolution_convert_fusion), channel_id=1, source_target_pairs={{0,4},{1,3},{4,8},{5,1},{8,12},{9,5},{12,14},{13,9},{14,10},{15,13... | collective-permute-start | bytes 1179656 | tf_op jit(solution)/shard_map/hop_sum/ppermute | solution.py:55
  20.6 10.7 %collective-permute-start.9 = (bf16[128,1536]{1,0:T(8,128)(2,1)S(1)}, bf16[128,1536]{1,0:T(8,128)(2,1)S(1)}, u32[]{:S(2)}, u32[]{:S(2)}) collective-permute-start(bf16[128,1536]{1,0:T(8,128)(2,1)S(1)} %collective-permute-done.6), channel_id=1, source_target_pairs={{0,4},{1,3},{4,8},{5,1},{8,12},{9,5},{12,14},{13,9},{14,10},{15,13... | collective-permute-start | bytes 1179656 | tf_op jit(solution)/shard_map/hop_x/ppermute | solution.py:55
  24.6 10.8 %collective-permute-start.5 = (bf16[128,1536]{1,0:T(8,128)(2,1)S(1)}, bf16[128,1536]{1,0:T(8,128)(2,1)S(1)}, u32[]{:S(2)}, u32[]{:S(2)}) collective-permute-start(bf16[128,1536]{1,0:T(8,128)(2,1)S(1)} %collective-permute-done.4), channel_id=1, source_target_pairs={{0,4},{1,3},{4,8},{5,1},{8,12},{9,5},{12,14},{13,9},{14,10},{15,13... | collective-permute-start | bytes 1179656 | tf_op jit(solution)/shard_map/hop_g/ppermute | solution.py:55
  27.6 12.0 %collective-permute-start.10 = (bf16[128,1536]{1,0:T(8,128)(2,1)S(1)}, bf16[128,1536]{1,0:T(8,128)(2,1)S(1)}, u32[]{:S(2)}, u32[]{:S(2)}) collective-permute-start(bf16[128,1536]{1,0:T(8,128)(2,1)S(1)} %fusion.4), channel_id=1, source_target_pairs={{0,4},{1,3},{4,8},{5,1},{8,12},{9,5},{12,14},{13,9},{14,10},{15,13... | collective-permute-start | bytes 1179656 | tf_op jit(solution)/shard_map/hop_sum/ppermute | solution.py:55
  32.2 11.7 %collective-permute-start.12 = (bf16[128,1536]{1,0:T(8,128)(2,1)S(1)}, bf16[128,1536]{1,0:T(8,128)(2,1)S(1)}, u32[]{:S(2)}, u32[]{:S(2)}) collective-permute-start(bf16[128,1536]{1,0:T(8,128)(2,1)S(1)} %collective-permute-done.9), channel_id=1, source_target_pairs={{0,4},{1,3},{4,8},{5,1},{8,12},{9,5},{12,14},{13,9},{14,10},{15,13... | collective-permute-start | bytes 1179656 | tf_op jit(solution)/shard_map/hop_x/ppermute | solution.py:55
  35.4 12.6 %collective-permute-start.8 = (bf16[128,1536]{1,0:T(8,128)(2,1)S(1)}, bf16[128,1536]{1,0:T(8,128)(2,1)S(1)}, u32[]{:S(2)}, u32[]{:S(2)}) collective-permute-start(bf16[128,1536]{1,0:T(8,128)(2,1)S(1)} %collective-permute-done.5), channel_id=1, source_target_pairs={{0,4},{1,3},{4,8},{5,1},{8,12},{9,5},{12,14},{13,9},{14,10},{15,13... | collective-permute-start | bytes 1179656 | tf_op jit(solution)/shard_map/hop_g/ppermute | solution.py:55
  40.1 12.2 %collective-permute-start.13 = (bf16[128,1536]{1,0:T(8,128)(2,1)S(1)}, bf16[128,1536]{1,0:T(8,128)(2,1)S(1)}, u32[]{:S(2)}, u32[]{:S(2)}) collective-permute-start(bf16[128,1536]{1,0:T(8,128)(2,1)S(1)} %fusion.5), channel_id=1, source_target_pairs={{0,4},{1,3},{4,8},{5,1},{8,12},{9,5},{12,14},{13,9},{14,10},{15,13... | collective-permute-start | bytes 1179656 | tf_op jit(solution)/shard_map/hop_sum/ppermute | solution.py:55
  44.8 15.3 %collective-permute-start.15 = (bf16[128,1536]{1,0:T(8,128)(2,1)S(1)}, bf16[128,1536]{1,0:T(8,128)(2,1)S(1)}, u32[]{:S(2)}, u32[]{:S(2)}) collective-permute-start(bf16[128,1536]{1,0:T(8,128)(2,1)S(1)} %collective-permute-done.12), channel_id=1, source_target_pairs={{0,4},{1,3},{4,8},{5,1},{8,12},{9,5},{12,14},{13,9},{14,10},{15,13... | collective-permute-start | bytes 1179656 | tf_op jit(solution)/shard_map/hop_x/ppermute | solution.py:55
  48.1 14.6 %collective-permute-start.11 = (bf16[128,1536]{1,0:T(8,128)(2,1)S(1)}, bf16[128,1536]{1,0:T(8,128)(2,1)S(1)}, u32[]{:S(2)}, u32[]{:S(2)}) collective-permute-start(bf16[128,1536]{1,0:T(8,128)(2,1)S(1)} %collective-permute-done.8), channel_id=1, source_target_pairs={{0,4},{1,3},{4,8},{5,1},{8,12},{9,5},{12,14},{13,9},{14,10},{15,13... | collective-permute-start | bytes 1179656 | tf_op jit(solution)/shard_map/hop_g/ppermute | solution.py:55
  52.8 12.4 %collective-permute-start.16 = (bf16[128,1536]{1,0:T(8,128)(2,1)S(1)}, bf16[128,1536]{1,0:T(8,128)(2,1)S(1)}, u32[]{:S(2)}, u32[]{:S(2)}) collective-permute-start(bf16[128,1536]{1,0:T(8,128)(2,1)S(1)} %fusion.6), channel_id=1, source_target_pairs={{0,4},{1,3},{4,8},{5,1},{8,12},{9,5},{12,14},{13,9},{14,10},{15,13... | collective-permute-start | bytes 1179656 | tf_op jit(solution)/shard_map/hop_sum/ppermute | solution.py:55
  61.0 8.5 %collective-permute-start.18 = (bf16[128,1536]{1,0:T(8,128)(2,1)S(1)}, bf16[128,1536]{1,0:T(8,128)(2,1)S(1)}, u32[]{:S(2)}, u32[]{:S(2)}) collective-permute-start(bf16[128,1536]{1,0:T(8,128)(2,1)S(1)} %collective-permute-done.15), channel_id=1, source_target_pairs={{0,4},{1,3},{4,8},{5,1},{8,12},{9,5},{12,14},{13,9},{14,10},{15,13... | collective-permute-start | bytes 1179656 | tf_op jit(solution)/shard_map/hop_x/ppermute | solution.py:55
  62.7 10.7 %collective-permute-start.14 = (bf16[128,1536]{1,0:T(8,128)(2,1)S(1)}, bf16[128,1536]{1,0:T(8,128)(2,1)S(1)}, u32[]{:S(2)}, u32[]{:S(2)}) collective-permute-start(bf16[128,1536]{1,0:T(8,128)(2,1)S(1)} %collective-permute-done.11), channel_id=1, source_target_pairs={{0,4},{1,3},{4,8},{5,1},{8,12},{9,5},{12,14},{13,9},{14,10},{15,13... | collective-permute-start | bytes 1179656 | tf_op jit(solution)/shard_map/hop_g/ppermute | solution.py:55
  65.7 11.9 %collective-permute-start.19 = (bf16[128,1536]{1,0:T(8,128)(2,1)S(1)}, bf16[128,1536]{1,0:T(8,128)(2,1)S(1)}, u32[]{:S(2)}, u32[]{:S(2)}) collective-permute-start(bf16[128,1536]{1,0:T(8,128)(2,1)S(1)} %fusion.7), channel_id=1, source_target_pairs={{0,4},{1,3},{4,8},{5,1},{8,12},{9,5},{12,14},{13,9},{14,10},{15,13... | collective-permute-start | bytes 1179656 | tf_op jit(solution)/shard_map/hop_sum/ppermute | solution.py:55
  69.5 12.3 %collective-permute-start.20 = (bf16[128,1536]{1,0:T(8,128)(2,1)S(1)}, bf16[128,1536]{1,0:T(8,128)(2,1)S(1)}, u32[]{:S(2)}, u32[]{:S(2)}) collective-permute-start(bf16[128,1536]{1,0:T(8,128)(2,1)S(1)} %collective-permute-done.18), channel_id=1, source_target_pairs={{0,4},{1,3},{4,8},{5,1},{8,12},{9,5},{12,14},{13,9},{14,10},{15,13... | collective-permute-start | bytes 1179656 | tf_op jit(solution)/shard_map/hop_x/ppermute | solution.py:55
  73.3 12.6 %collective-permute-start.17 = (bf16[128,1536]{1,0:T(8,128)(2,1)S(1)}, bf16[128,1536]{1,0:T(8,128)(2,1)S(1)}, u32[]{:S(2)}, u32[]{:S(2)}) collective-permute-start(bf16[128,1536]{1,0:T(8,128)(2,1)S(1)} %collective-permute-done.14), channel_id=1, source_target_pairs={{0,4},{1,3},{4,8},{5,1},{8,12},{9,5},{12,14},{13,9},{14,10},{15,13... | collective-permute-start | bytes 1179656 | tf_op jit(solution)/shard_map/hop_g/ppermute | solution.py:55
  78.0 12.2 %collective-permute-start.21 = (bf16[128,1536]{1,0:T(8,128)(2,1)S(1)}, bf16[128,1536]{1,0:T(8,128)(2,1)S(1)}, u32[]{:S(2)}, u32[]{:S(2)}) collective-permute-start(bf16[128,1536]{1,0:T(8,128)(2,1)S(1)} %fusion.8), channel_id=1, source_target_pairs={{0,4},{1,3},{4,8},{5,1},{8,12},{9,5},{12,14},{13,9},{14,10},{15,13... | collective-permute-start | bytes 1179656 | tf_op jit(solution)/shard_map/hop_sum/ppermute | solution.py:55
  90.2 3.1 %collective-permute-start.23 = (bf16[384,1536]{1,0:T(8,128)(2,1)S(1)}, bf16[384,1536]{1,0:T(8,128)(2,1)S(1)}, u32[]{:S(2)}, u32[]{:S(2)}) collective-permute-start(bf16[384,1536]{1,0:T(8,128)(2,1)S(1)} %fusion.2), channel_id=1, source_target_pairs={{0,1},{1,0},{2,3},{3,2},{4,5},{5,4},{6,7},{7,6},{8,9},{9,8},{10,11... | collective-permute-start | bytes 3538952 | tf_op jit(solution)/shard_map/swap_grads/ppermute | solution.py:59
  90.2 5.0 %collective-permute-start.24 = (bf16[384,1536]{1,0:T(8,128)(2,1)S(1)}, bf16[384,1536]{1,0:T(8,128)(2,1)S(1)}, u32[]{:S(2)}, u32[]{:S(2)}) collective-permute-start(bf16[384,1536]{1,0:T(8,128)(2,1)S(1)} %fusion.3), channel_id=1, source_target_pairs={{0,1},{1,0},{2,3},{3,2},{4,5},{5,4},{6,7},{7,6},{8,9},{9,8},{10,11... | collective-permute-start | bytes 3538952 | tf_op jit(solution)/shard_map/swap_grads/ppermute | solution.py:59
  91.2 7.8 %collective-permute-start.22 = (bf16[128,1536]{1,0:T(8,128)(2,1)S(1)}, bf16[128,1536]{1,0:T(8,128)(2,1)S(1)}, u32[]{:S(2)}, u32[]{:S(2)}) collective-permute-start(bf16[128,1536]{1,0:T(8,128)(2,1)S(1)} %fusion.9), channel_id=1, source_target_pairs={{0,4},{1,3},{4,8},{5,1},{8,12},{9,5},{12,14},{13,9},{14,10},{15,13... | collective-permute-start | bytes 1179656 | tf_op jit(solution)/shard_map/hop_sum/ppermute | solution.py:55

commit v3 on v2

--- a/solution.py
+++ b/solution.py
@@ -71,6 +71,11 @@
     up_rows = jnp.concatenate([up_weight, across(up_weight, "swap_up")], axis=0)
     down_rows = jnp.concatenate([down_weight, across(down_weight, "swap_down")], axis=0)
 
+    width = up_rows.shape[1]
+    span = width // 2
+    starts = range(0, width, span)
+    up_cuts = [up_rows[:, at:at + span] for at in starts]
+
     def middle(x, g):
         value, slope = gelu_pair(dot(x, up_rows, LAST))
         hidden = value.astype(jnp.bfloat16)
@@ -96,15 +101,23 @@
             with jax.named_scope("last"):
                 mine = add(mine, gradients(waiting, own))
                 theirs = [a.astype(jnp.bfloat16) for a in add(theirs, gradients(waiting, other))]
-            carried = behind(carried, waiting[-1], theirs)
+            carried = [behind(part, waiting[-1], theirs) for part in carried]
         with jax.named_scope("token_part"):
-            total = dot(waiting[-1][3], up_rows, ROWS)
+            if step < chips - 2:
+                totals = [dot(waiting[-1][3], up_rows, ROWS)]
+            else:
+                totals = [dot(waiting[-1][3], columns, ROWS) for columns in up_cuts]
+            if step == chips - 2:
+                carried = [carried[0][:, at:at + span] for at in starts]
             if carried is not None:
-                total = total + carried.astype(jnp.float32)
-            total = total.astype(jnp.bfloat16)
+                totals = [a + b.astype(jnp.float32) for a, b in zip(totals, carried)]
+            totals = [a.astype(jnp.bfloat16) for a in totals]
         arrived = carried
-        carried = hop(total, "hop_sum")
-        done = [total]
+        if step == chips - 1:
+            pass
+        carried = [hop(total, "hop_sum") for total in totals]
+        total = totals[0]
+        done = list(totals)
         if step == 1:
             waiting.append(middle(behind(tokens, total), weighted))
             base = weighted.astype(jnp.float32) + dot(waiting[-1][3], up_rows, ROWS)
@@ -121,11 +134,18 @@
         if step < chips - 1:
             x_next, g_next = behind(x_next, *done), behind(g_next, *done)
 
-    received = [across(behind(a, arrived), "swap_grads") for a in theirs]
+    received = [across(behind(a, arrived[0]), "swap_grads") for a in theirs]
     with jax.named_scope("finish"):
+        mine = [behind(a, carried[0]) for a in mine]
         grad_up, grad_down = [a + b.astype(jnp.float32) for a, b in zip(mine, received)]
         carried, grad_up, grad_down = lax.optimization_barrier((carried, grad_up, grad_down))
-        grad_tokens = (base + carried.astype(jnp.float32)).astype(jnp.bfloat16)
+        grad_tokens = jnp.concatenate(
+            [
+                (base[:, at:at + span] + part.astype(jnp.float32)).astype(jnp.bfloat16)
+                for at, part in zip(starts, carried)
+            ],
+            axis=1,
+        )
     return grad_tokens, grad_up, grad_down
 
 

time: 100 us -> 98.7 us (0.987)
  waiting for transfers between devices: 21.1 us -> 15.8 us
  other arithmetic: 2.71 us -> 6.21 us
  starting transfers between devices: 42.7 us -> 45.6 us
  matrix products: 30.1 us -> 27.6 us
    ppermute x21 -> x23, waiting for transfers between devices: 21.1 us -> 15.8 us  [hop(): return lax.ppermute(block, 'gx', route)]
    add x0 -> x2, other arithmetic: none -> 3.47 us  [local(): a + b.astype(jnp.float32)]
    ppermute x21 -> x23, starting transfers between devices: 41.6 us -> 44.8 us  [hop(): return lax.ppermute(block, 'gx', route)]
    dot_general x36 -> x38, matrix products: 30.1 us -> 27.6 us  [dot(): return lax.dot_general(a, b, dims, preferred_element_type=jnp.float32)]
  transfers between devices with their start and end apart: 25 -> 27, of which waited for: 14 -> 13; matrix products, arithmetic and copies ran while one was open for 34% -> 36% of each run, Pallas kernels for 0% -> 0%
where the time goes in v3:
time: 98.7 us; the launch traced here: 98.5 us
  starting transfers between devices  45.6 us (46%)
  matrix products  27.6 us (28%)
  waiting for transfers between devices  15.8 us (16%)
  other arithmetic  6.21 us (6%)
  local copies, waits for them, and re-layouts  2.12 us (2%)
  between operations  1.15 us (1%)
    ppermute x23, starting transfers between devices, hop(): return lax.ppermute(block, 'gx', route)  44.8 us
    dot_general x38, matrix products, dot(): return lax.dot_general(a, b, dims, preferred_element_type=jnp.float32)  27.6 us
    ppermute x23, waiting for transfers between devices, hop(): return lax.ppermute(block, 'gx', route)  15.8 us
    add x2, other arithmetic, local(): a + b.astype(jnp.float32)  3.47 us
  transfers between devices with their start and end apart: 27, of which 13 were waited for; matrix products, arithmetic and copies ran while one was open for 36% of the time, Pallas kernels for 0%

profile of v3, /device:TPU:0, one launch (start us, length us, event | category | flops | bytes accessed | tf_op | source)
XLA Modules:
  0.0 98.5 jit_solution(3124477584018346196)
XLA Ops:
  1.2 3.0 %collective-permute-start.3 = (bf16[128,1536]{1,0:T(8,128)(2,1)}, bf16[128,1536]{1,0:T(8,128)(2,1)S(1)}, u32[]{:S(2)}, u32[]{:S(2)}) collective-permute-start(bf16[128,1536]{1,0:T(8,128)(2,1)} %param.6), channel_id=1, source_target_pairs={{0,4},{1,3},{4,8},{5,1},{8,12},{9,5},{12,14},{13,9},{14,10},{15,13... | collective-permute-start | bytes 1179656 | tf_op jit(solution)/shard_map/hop_x/ppermute | solution.py:55
  6.1 1.6 %collective-permute-start.1 = (bf16[128,1536]{1,0:T(8,128)(2,1)S(1)}, bf16[128,1536]{1,0:T(8,128)(2,1)S(1)}, u32[]{:S(2)}, u32[]{:S(2)}) collective-permute-start(bf16[128,1536]{1,0:T(8,128)(2,1)S(1)} %multiply_convert_fusion), channel_id=1, source_target_pairs={{0,4},{1,3},{4,8},{5,1},{8,12},{9,5},{12,14},{13,9},{14,10},{15,13... | collective-permute-start | bytes 1179656 | tf_op jit(solution)/shard_map/hop_g/ppermute | solution.py:55
  7.8 1.3 %constant_dynamic-update-slice_fusion.1 = bf16[768,1536]{1,0:T(8,128)(2,1)S(1)} fusion(bf16[384,1536]{1,0:T(8,128)(2,1)} %param.11), kind=kLoop, calls=%fused_computation.144 | loop fusion | bytes 2359296
  10.1 2.1 %collective-permute-start.6 = (bf16[128,1536]{1,0:T(8,128)(2,1)S(1)}, bf16[128,1536]{1,0:T(8,128)(2,1)S(1)}, u32[]{:S(2)}, u32[]{:S(2)}) collective-permute-start(bf16[128,1536]{1,0:T(8,128)(2,1)S(1)} %collective-permute-done.3), channel_id=1, source_target_pairs={{0,4},{1,3},{4,8},{5,1},{8,12},{9,5},{12,14},{13,9},{14,10},{15,13... | collective-permute-start | bytes 1179656 | tf_op jit(solution)/shard_map/hop_x/ppermute | solution.py:55
  14.4 2.1 %collective-permute-start.4 = (bf16[128,1536]{1,0:T(8,128)(2,1)S(1)}, bf16[128,1536]{1,0:T(8,128)(2,1)S(1)}, u32[]{:S(2)}, u32[]{:S(2)}) collective-permute-start(bf16[128,1536]{1,0:T(8,128)(2,1)S(1)} %collective-permute-done.1), channel_id=1, source_target_pairs={{0,4},{1,3},{4,8},{5,1},{8,12},{9,5},{12,14},{13,9},{14,10},{15,13... | collective-permute-start | bytes 1179656 | tf_op jit(solution)/shard_map/hop_g/ppermute | solution.py:55
  18.0 1.6 %collective-permute-start.7 = (bf16[128,1536]{1,0:T(8,128)(2,1)S(1)}, bf16[128,1536]{1,0:T(8,128)(2,1)S(1)}, u32[]{:S(2)}, u32[]{:S(2)}) collective-permute-start(bf16[128,1536]{1,0:T(8,128)(2,1)S(1)} %convolution_convert_fusion), channel_id=1, source_target_pairs={{0,4},{1,3},{4,8},{5,1},{8,12},{9,5},{12,14},{13,9},{14,10},{15,13... | collective-permute-start | bytes 1179656 | tf_op jit(solution)/shard_map/hop_sum/ppermute | solution.py:55
  20.6 1.6 %collective-permute-start.9 = (bf16[128,1536]{1,0:T(8,128)(2,1)S(1)}, bf16[128,1536]{1,0:T(8,128)(2,1)S(1)}, u32[]{:S(2)}, u32[]{:S(2)}) collective-permute-start(bf16[128,1536]{1,0:T(8,128)(2,1)S(1)} %collective-permute-done.6), channel_id=1, source_target_pairs={{0,4},{1,3},{4,8},{5,1},{8,12},{9,5},{12,14},{13,9},{14,10},{15,13... | collective-permute-start | bytes 1179656 | tf_op jit(solution)/shard_map/hop_x/ppermute | solution.py:55
  24.6 1.6 %collective-permute-start.5 = (bf16[128,1536]{1,0:T(8,128)(2,1)S(1)}, bf16[128,1536]{1,0:T(8,128)(2,1)S(1)}, u32[]{:S(2)}, u32[]{:S(2)}) collective-permute-start(bf16[128,1536]{1,0:T(8,128)(2,1)S(1)} %collective-permute-done.4), channel_id=1, source_target_pairs={{0,4},{1,3},{4,8},{5,1},{8,12},{9,5},{12,14},{13,9},{14,10},{15,13... | collective-permute-start | bytes 1179656 | tf_op jit(solution)/shard_map/hop_g/ppermute | solution.py:55
  27.6 2.0 %collective-permute-start.10 = (bf16[128,1536]{1,0:T(8,128)(2,1)S(1)}, bf16[128,1536]{1,0:T(8,128)(2,1)S(1)}, u32[]{:S(2)}, u32[]{:S(2)}) collective-permute-start(bf16[128,1536]{1,0:T(8,128)(2,1)S(1)} %fusion.2), channel_id=1, source_target_pairs={{0,4},{1,3},{4,8},{5,1},{8,12},{9,5},{12,14},{13,9},{14,10},{15,13... | collective-permute-start | bytes 1179656 | tf_op jit(solution)/shard_map/hop_sum/ppermute | solution.py:55
  29.6 1.6 %collective-permute-done.9 = bf16[128,1536]{1,0:T(8,128)(2,1)S(1)} collective-permute-done((bf16[128,1536]{1,0:T(8,128)(2,1)S(1)}, bf16[128,1536]{1,0:T(8,128)(2,1)S(1)}, u32[]{:S(2)}, u32[]{:S(2)}) %collective-permute-start.9) | collective-permute-done | bytes 393248 | tf_op jit(solution)/shard_map/hop_x/ppermute | solution.py:55
  32.2 2.1 %collective-permute-start.12 = (bf16[128,1536]{1,0:T(8,128)(2,1)S(1)}, bf16[128,1536]{1,0:T(8,128)(2,1)S(1)}, u32[]{:S(2)}, u32[]{:S(2)}) collective-permute-start(bf16[128,1536]{1,0:T(8,128)(2,1)S(1)} %collective-permute-done.9), channel_id=1, source_target_pairs={{0,4},{1,3},{4,8},{5,1},{8,12},{9,5},{12,14},{13,9},{14,10},{15,13... | collective-permute-start | bytes 1179656 | tf_op jit(solution)/shard_map/hop_x/ppermute | solution.py:55
  35.4 2.1 %collective-permute-start.8 = (bf16[128,1536]{1,0:T(8,128)(2,1)S(1)}, bf16[128,1536]{1,0:T(8,128)(2,1)S(1)}, u32[]{:S(2)}, u32[]{:S(2)}) collective-permute-start(bf16[128,1536]{1,0:T(8,128)(2,1)S(1)} %collective-permute-done.5), channel_id=1, source_target_pairs={{0,4},{1,3},{4,8},{5,1},{8,12},{9,5},{12,14},{13,9},{14,10},{15,13... | collective-permute-start | bytes 1179656 | tf_op jit(solution)/shard_map/hop_g/ppermute | solution.py:55
  38.5 1.2 %collective-permute-done.10 = bf16[128,1536]{1,0:T(8,128)(2,1)S(1)} collective-permute-done((bf16[128,1536]{1,0:T(8,128)(2,1)S(1)}, bf16[128,1536]{1,0:T(8,128)(2,1)S(1)}, u32[]{:S(2)}, u32[]{:S(2)}) %collective-permute-start.10) | collective-permute-done | bytes 393248 | tf_op jit(solution)/shard_map/hop_sum/ppermute | solution.py:55
  40.1 2.1 %collective-permute-start.13 = (bf16[128,1536]{1,0:T(8,128)(2,1)S(1)}, bf16[128,1536]{1,0:T(8,128)(2,1)S(1)}, u32[]{:S(2)}, u32[]{:S(2)}) collective-permute-start(bf16[128,1536]{1,0:T(8,128)(2,1)S(1)} %fusion.3), channel_id=1, source_target_pairs={{0,4},{1,3},{4,8},{5,1},{8,12},{9,5},{12,14},{13,9},{14,10},{15,13... | collective-permute-start | bytes 1179656 | tf_op jit(solution)/shard_map/hop_sum/ppermute | solution.py:55
  42.3 1.6 %collective-permute-done.12 = bf16[128,1536]{1,0:T(8,128)(2,1)S(1)} collective-permute-done((bf16[128,1536]{1,0:T(8,128)(2,1)S(1)}, bf16[128,1536]{1,0:T(8,128)(2,1)S(1)}, u32[]{:S(2)}, u32[]{:S(2)}) %collective-permute-start.12) | collective-permute-done | bytes 393248 | tf_op jit(solution)/shard_map/hop_x/ppermute | solution.py:55
  44.8 2.1 %collective-permute-start.15 = (bf16[128,1536]{1,0:T(8,128)(2,1)S(1)}, bf16[128,1536]{1,0:T(8,128)(2,1)S(1)}, u32[]{:S(2)}, u32[]{:S(2)}) collective-permute-start(bf16[128,1536]{1,0:T(8,128)(2,1)S(1)} %collective-permute-done.12), channel_id=1, source_target_pairs={{0,4},{1,3},{4,8},{5,1},{8,12},{9,5},{12,14},{13,9},{14,10},{15,13... | collective-permute-start | bytes 1179656 | tf_op jit(solution)/shard_map/hop_x/ppermute | solution.py:55
  48.1 2.1 %collective-permute-start.11 = (bf16[128,1536]{1,0:T(8,128)(2,1)S(1)}, bf16[128,1536]{1,0:T(8,128)(2,1)S(1)}, u32[]{:S(2)}, u32[]{:S(2)}) collective-permute-start(bf16[128,1536]{1,0:T(8,128)(2,1)S(1)} %collective-permute-done.8), channel_id=1, source_target_pairs={{0,4},{1,3},{4,8},{5,1},{8,12},{9,5},{12,14},{13,9},{14,10},{15,13... | collective-permute-start | bytes 1179656 | tf_op jit(solution)/shard_map/hop_g/ppermute | solution.py:55
  51.1 1.2 %collective-permute-done.13 = bf16[128,1536]{1,0:T(8,128)(2,1)S(1)} collective-permute-done((bf16[128,1536]{1,0:T(8,128)(2,1)S(1)}, bf16[128,1536]{1,0:T(8,128)(2,1)S(1)}, u32[]{:S(2)}, u32[]{:S(2)}) %collective-permute-start.13) | collective-permute-done | bytes 393248 | tf_op jit(solution)/shard_map/hop_sum/ppermute | solution.py:55
  52.8 2.3 %collective-permute-start.16 = (bf16[128,1536]{1,0:T(8,128)(2,1)S(1)}, bf16[128,1536]{1,0:T(8,128)(2,1)S(1)}, u32[]{:S(2)}, u32[]{:S(2)}) collective-permute-start(bf16[128,1536]{1,0:T(8,128)(2,1)S(1)} %fusion.4), channel_id=1, source_target_pairs={{0,4},{1,3},{4,8},{5,1},{8,12},{9,5},{12,14},{13,9},{14,10},{15,13... | collective-permute-start | bytes 1179656 | tf_op jit(solution)/shard_map/hop_sum/ppermute | solution.py:55
  61.0 1.6 %collective-permute-start.18 = (bf16[128,1536]{1,0:T(8,128)(2,1)S(1)}, bf16[128,1536]{1,0:T(8,128)(2,1)S(1)}, u32[]{:S(2)}, u32[]{:S(2)}) collective-permute-start(bf16[128,1536]{1,0:T(8,128)(2,1)S(1)} %collective-permute-done.15), channel_id=1, source_target_pairs={{0,4},{1,3},{4,8},{5,1},{8,12},{9,5},{12,14},{13,9},{14,10},{15,13... | collective-permute-start | bytes 1179656 | tf_op jit(solution)/shard_map/hop_x/ppermute | solution.py:55
  62.7 1.6 %collective-permute-start.14 = (bf16[128,1536]{1,0:T(8,128)(2,1)S(1)}, bf16[128,1536]{1,0:T(8,128)(2,1)S(1)}, u32[]{:S(2)}, u32[]{:S(2)}) collective-permute-start(bf16[128,1536]{1,0:T(8,128)(2,1)S(1)} %collective-permute-done.11), channel_id=1, source_target_pairs={{0,4},{1,3},{4,8},{5,1},{8,12},{9,5},{12,14},{13,9},{14,10},{15,13... | collective-permute-start | bytes 1179656 | tf_op jit(solution)/shard_map/hop_g/ppermute | solution.py:55
  65.7 1.9 %collective-permute-start.19 = (bf16[128,1536]{1,0:T(8,128)(2,1)S(1)}, bf16[128,1536]{1,0:T(8,128)(2,1)S(1)}, u32[]{:S(2)}, u32[]{:S(2)}) collective-permute-start(bf16[128,1536]{1,0:T(8,128)(2,1)S(1)} %fusion.5), channel_id=1, source_target_pairs={{0,4},{1,3},{4,8},{5,1},{8,12},{9,5},{12,14},{13,9},{14,10},{15,13... | collective-permute-start | bytes 1179656 | tf_op jit(solution)/shard_map/hop_sum/ppermute | solution.py:55
  69.5 1.7 %collective-permute-start.20 = (bf16[128,1536]{1,0:T(8,128)(2,1)S(1)}, bf16[128,1536]{1,0:T(8,128)(2,1)S(1)}, u32[]{:S(2)}, u32[]{:S(2)}) collective-permute-start(bf16[128,1536]{1,0:T(8,128)(2,1)S(1)} %collective-permute-done.18), channel_id=1, source_target_pairs={{0,4},{1,3},{4,8},{5,1},{8,12},{9,5},{12,14},{13,9},{14,10},{15,13... | collective-permute-start | bytes 1179656 | tf_op jit(solution)/shard_map/hop_x/ppermute | solution.py:55
  73.3 2.1 %collective-permute-start.17 = (bf16[128,1536]{1,0:T(8,128)(2,1)S(1)}, bf16[128,1536]{1,0:T(8,128)(2,1)S(1)}, u32[]{:S(2)}, u32[]{:S(2)}) collective-permute-start(bf16[128,1536]{1,0:T(8,128)(2,1)S(1)} %collective-permute-done.14), channel_id=1, source_target_pairs={{0,4},{1,3},{4,8},{5,1},{8,12},{9,5},{12,14},{13,9},{14,10},{15,13... | collective-permute-start | bytes 1179656 | tf_op jit(solution)/shard_map/hop_g/ppermute | solution.py:55
  76.4 1.2 %collective-permute-done.19 = bf16[128,1536]{1,0:T(8,128)(2,1)S(1)} collective-permute-done((bf16[128,1536]{1,0:T(8,128)(2,1)S(1)}, bf16[128,1536]{1,0:T(8,128)(2,1)S(1)}, u32[]{:S(2)}, u32[]{:S(2)}) %collective-permute-start.19) | collective-permute-done | bytes 393248 | tf_op jit(solution)/shard_map/hop_sum/ppermute | solution.py:55
  77.9 2.1 %collective-permute-start.21 = (bf16[128,768]{1,0:T(8,128)(2,1)S(1)}, bf16[128,768]{1,0:T(8,128)(2,1)S(1)}, u32[]{:S(2)}, u32[]{:S(2)}) collective-permute-start(bf16[128,768]{1,0:T(8,128)(2,1)S(1)} %fusion.6), channel_id=1, source_target_pairs={{0,4},{1,3},{4,8},{5,1},{8,12},{9,5},{12,14},{13,9},{14,10},{15,13... | collective-permute-start | bytes 589832 | tf_op jit(solution)/shard_map/hop_sum/ppermute | solution.py:55
  80.4 1.6 %collective-permute-start.23 = (bf16[128,768]{1,0:T(8,128)(2,1)S(1)}, bf16[128,768]{1,0:T(8,128)(2,1)S(1)}, u32[]{:S(2)}, u32[]{:S(2)}) collective-permute-start(bf16[128,768]{1,0:T(8,128)(2,1)S(1)} %fusion.7), channel_id=1, source_target_pairs={{0,4},{1,3},{4,8},{5,1},{8,12},{9,5},{12,14},{13,9},{14,10},{15,13... | collective-permute-start | bytes 589832 | tf_op jit(solution)/shard_map/hop_sum/ppermute | solution.py:55
  83.0 3.0 %collective-permute-done.17 = bf16[128,1536]{1,0:T(8,128)(2,1)S(1)} collective-permute-done((bf16[128,1536]{1,0:T(8,128)(2,1)S(1)}, bf16[128,1536]{1,0:T(8,128)(2,1)S(1)}, u32[]{:S(2)}, u32[]{:S(2)}) %collective-permute-start.17) | collective-permute-done | bytes 393248 | tf_op jit(solution)/shard_map/hop_g/ppermute | solution.py:55
  88.4 2.1 %collective-permute-start.22 = (bf16[128,768]{1,0:T(8,128)(2,1)S(1)}, bf16[128,768]{1,0:T(8,128)(2,1)S(1)}, u32[]{:S(2)}, u32[]{:S(2)}) collective-permute-start(bf16[128,768]{1,0:T(8,128)(2,1)S(1)} %fusion.8), channel_id=1, source_target_pairs={{0,4},{1,3},{4,8},{5,1},{8,12},{9,5},{12,14},{13,9},{14,10},{15,13... | collective-permute-start | bytes 589832 | tf_op jit(solution)/shard_map/hop_sum/ppermute | solution.py:55
  91.6 1.6 %collective-permute-start.24 = (bf16[128,768]{1,0:T(8,128)(2,1)S(1)}, bf16[128,768]{1,0:T(8,128)(2,1)S(1)}, u32[]{:S(2)}, u32[]{:S(2)}) collective-permute-start(bf16[128,768]{1,0:T(8,128)(2,1)S(1)} %fusion.9), channel_id=1, source_target_pairs={{0,4},{1,3},{4,8},{5,1},{8,12},{9,5},{12,14},{13,9},{14,10},{15,13... | collective-permute-start | bytes 589832 | tf_op jit(solution)/shard_map/hop_sum/ppermute | solution.py:55
  94.2 1.7 %convert_add_fusion.1 = f32[384,1536]{1,0:T(8,128)} fusion(f32[384,1536]{1,0:T(8,128)S(1)} %convolution_add_fusion.1, bf16[384,1536]{1,0:T(8,128)(2,1)S(1)} %collective-permute-done.25), kind=kLoop, calls=%fused_computation.21 | loop fusion | flops 1179648 | bytes 5898240 | tf_op jit(solution)/shard_map/finish/add | solution.py:140
  95.9 1.7 %convert_add_fusion = f32[384,1536]{1,0:T(8,128)} fusion(f32[384,1536]{1,0:T(8,128)S(1)} %convolution_add_fusion, bf16[384,1536]{1,0:T(8,128)(2,1)S(1)} %collective-permute-done.26), kind=kLoop, calls=%fused_computation.20 | loop fusion | flops 1179648 | bytes 5898240 | tf_op jit(solution)/shard_map/finish/add | solution.py:140
  (97 shorter events, 38.0 us)
Async XLA Ops:
  0.6 8.5 %copy-start.1 = (bf16[384,1536]{1,0:T(8,128)(2,1)S(1)}, bf16[384,1536]{1,0:T(8,128)(2,1)}, u32[]{:S(2)}) copy-start(bf16[384,1536]{1,0:T(8,128)(2,1)} %param.10) | copy-start | bytes 3538948
  0.6 15.8 %collective-permute-start = (bf16[384,1536]{1,0:T(8,128)(2,1)}, bf16[384,1536]{1,0:T(8,128)(2,1)S(1)}, u32[]{:S(2)}, u32[]{:S(2)}) collective-permute-start(bf16[384,1536]{1,0:T(8,128)(2,1)} %param.11), channel_id=1, source_target_pairs={{0,1},{1,0},{2,3},{3,2},{4,5},{5,4},{6,7},{7,6},{8,9},{9,8},{10,11... | collective-permute-start | bytes 3538952 | tf_op jit(solution)/shard_map/swap_down/ppermute | solution.py:59
  1.2 11.1 %collective-permute-start.2 = (bf16[384,1536]{1,0:T(8,128)(2,1)}, bf16[384,1536]{1,0:T(8,128)(2,1)S(1)}, u32[]{:S(2)}, u32[]{:S(2)}) collective-permute-start(bf16[384,1536]{1,0:T(8,128)(2,1)} %param.10), channel_id=1, source_target_pairs={{0,1},{1,0},{2,3},{3,2},{4,5},{5,4},{6,7},{7,6},{8,9},{9,8},{10,11... | collective-permute-start | bytes 3538952 | tf_op jit(solution)/shard_map/swap_up/ppermute | solution.py:59
  1.2 8.9 %collective-permute-start.3 = (bf16[128,1536]{1,0:T(8,128)(2,1)}, bf16[128,1536]{1,0:T(8,128)(2,1)S(1)}, u32[]{:S(2)}, u32[]{:S(2)}) collective-permute-start(bf16[128,1536]{1,0:T(8,128)(2,1)} %param.6), channel_id=1, source_target_pairs={{0,4},{1,3},{4,8},{5,1},{8,12},{9,5},{12,14},{13,9},{14,10},{15,13... | collective-permute-start | bytes 1179656 | tf_op jit(solution)/shard_map/hop_x/ppermute | solution.py:55
  6.1 8.2 %collective-permute-start.1 = (bf16[128,1536]{1,0:T(8,128)(2,1)S(1)}, bf16[128,1536]{1,0:T(8,128)(2,1)S(1)}, u32[]{:S(2)}, u32[]{:S(2)}) collective-permute-start(bf16[128,1536]{1,0:T(8,128)(2,1)S(1)} %multiply_convert_fusion), channel_id=1, source_target_pairs={{0,4},{1,3},{4,8},{5,1},{8,12},{9,5},{12,14},{13,9},{14,10},{15,13... | collective-permute-start | bytes 1179656 | tf_op jit(solution)/shard_map/hop_g/ppermute | solution.py:55
  10.1 9.5 %collective-permute-start.6 = (bf16[128,1536]{1,0:T(8,128)(2,1)S(1)}, bf16[128,1536]{1,0:T(8,128)(2,1)S(1)}, u32[]{:S(2)}, u32[]{:S(2)}) collective-permute-start(bf16[128,1536]{1,0:T(8,128)(2,1)S(1)} %collective-permute-done.3), channel_id=1, source_target_pairs={{0,4},{1,3},{4,8},{5,1},{8,12},{9,5},{12,14},{13,9},{14,10},{15,13... | collective-permute-start | bytes 1179656 | tf_op jit(solution)/shard_map/hop_x/ppermute | solution.py:55
  14.4 10.2 %collective-permute-start.4 = (bf16[128,1536]{1,0:T(8,128)(2,1)S(1)}, bf16[128,1536]{1,0:T(8,128)(2,1)S(1)}, u32[]{:S(2)}, u32[]{:S(2)}) collective-permute-start(bf16[128,1536]{1,0:T(8,128)(2,1)S(1)} %collective-permute-done.1), channel_id=1, source_target_pairs={{0,4},{1,3},{4,8},{5,1},{8,12},{9,5},{12,14},{13,9},{14,10},{15,13... | collective-permute-start | bytes 1179656 | tf_op jit(solution)/shard_map/hop_g/ppermute | solution.py:55
  18.0 4.2 %copy-start = (bf16[128,1536]{1,0:T(8,128)(2,1)S(1)}, bf16[128,1536]{1,0:T(8,128)(2,1)}, u32[]{:S(2)}) copy-start(bf16[128,1536]{1,0:T(8,128)(2,1)} %param.6) | copy-start | bytes 1179652
  18.0 9.1 %collective-permute-start.7 = (bf16[128,1536]{1,0:T(8,128)(2,1)S(1)}, bf16[128,1536]{1,0:T(8,128)(2,1)S(1)}, u32[]{:S(2)}, u32[]{:S(2)}) collective-permute-start(bf16[128,1536]{1,0:T(8,128)(2,1)S(1)} %convolution_convert_fusion), channel_id=1, source_target_pairs={{0,4},{1,3},{4,8},{5,1},{8,12},{9,5},{12,14},{13,9},{14,10},{15,13... | collective-permute-start | bytes 1179656 | tf_op jit(solution)/shard_map/hop_sum/ppermute | solution.py:55
  20.6 10.7 %collective-permute-start.9 = (bf16[128,1536]{1,0:T(8,128)(2,1)S(1)}, bf16[128,1536]{1,0:T(8,128)(2,1)S(1)}, u32[]{:S(2)}, u32[]{:S(2)}) collective-permute-start(bf16[128,1536]{1,0:T(8,128)(2,1)S(1)} %collective-permute-done.6), channel_id=1, source_target_pairs={{0,4},{1,3},{4,8},{5,1},{8,12},{9,5},{12,14},{13,9},{14,10},{15,13... | collective-permute-start | bytes 1179656 | tf_op jit(solution)/shard_map/hop_x/ppermute | solution.py:55
  24.6 10.8 %collective-permute-start.5 = (bf16[128,1536]{1,0:T(8,128)(2,1)S(1)}, bf16[128,1536]{1,0:T(8,128)(2,1)S(1)}, u32[]{:S(2)}, u32[]{:S(2)}) collective-permute-start(bf16[128,1536]{1,0:T(8,128)(2,1)S(1)} %collective-permute-done.4), channel_id=1, source_target_pairs={{0,4},{1,3},{4,8},{5,1},{8,12},{9,5},{12,14},{13,9},{14,10},{15,13... | collective-permute-start | bytes 1179656 | tf_op jit(solution)/shard_map/hop_g/ppermute | solution.py:55
  27.6 12.0 %collective-permute-start.10 = (bf16[128,1536]{1,0:T(8,128)(2,1)S(1)}, bf16[128,1536]{1,0:T(8,128)(2,1)S(1)}, u32[]{:S(2)}, u32[]{:S(2)}) collective-permute-start(bf16[128,1536]{1,0:T(8,128)(2,1)S(1)} %fusion.2), channel_id=1, source_target_pairs={{0,4},{1,3},{4,8},{5,1},{8,12},{9,5},{12,14},{13,9},{14,10},{15,13... | collective-permute-start | bytes 1179656 | tf_op jit(solution)/shard_map/hop_sum/ppermute | solution.py:55
  32.2 11.7 %collective-permute-start.12 = (bf16[128,1536]{1,0:T(8,128)(2,1)S(1)}, bf16[128,1536]{1,0:T(8,128)(2,1)S(1)}, u32[]{:S(2)}, u32[]{:S(2)}) collective-permute-start(bf16[128,1536]{1,0:T(8,128)(2,1)S(1)} %collective-permute-done.9), channel_id=1, source_target_pairs={{0,4},{1,3},{4,8},{5,1},{8,12},{9,5},{12,14},{13,9},{14,10},{15,13... | collective-permute-start | bytes 1179656 | tf_op jit(solution)/shard_map/hop_x/ppermute | solution.py:55
  35.4 12.6 %collective-permute-start.8 = (bf16[128,1536]{1,0:T(8,128)(2,1)S(1)}, bf16[128,1536]{1,0:T(8,128)(2,1)S(1)}, u32[]{:S(2)}, u32[]{:S(2)}) collective-permute-start(bf16[128,1536]{1,0:T(8,128)(2,1)S(1)} %collective-permute-done.5), channel_id=1, source_target_pairs={{0,4},{1,3},{4,8},{5,1},{8,12},{9,5},{12,14},{13,9},{14,10},{15,13... | collective-permute-start | bytes 1179656 | tf_op jit(solution)/shard_map/hop_g/ppermute | solution.py:55
  40.1 12.2 %collective-permute-start.13 = (bf16[128,1536]{1,0:T(8,128)(2,1)S(1)}, bf16[128,1536]{1,0:T(8,128)(2,1)S(1)}, u32[]{:S(2)}, u32[]{:S(2)}) collective-permute-start(bf16[128,1536]{1,0:T(8,128)(2,1)S(1)} %fusion.3), channel_id=1, source_target_pairs={{0,4},{1,3},{4,8},{5,1},{8,12},{9,5},{12,14},{13,9},{14,10},{15,13... | collective-permute-start | bytes 1179656 | tf_op jit(solution)/shard_map/hop_sum/ppermute | solution.py:55
  44.8 15.3 %collective-permute-start.15 = (bf16[128,1536]{1,0:T(8,128)(2,1)S(1)}, bf16[128,1536]{1,0:T(8,128)(2,1)S(1)}, u32[]{:S(2)}, u32[]{:S(2)}) collective-permute-start(bf16[128,1536]{1,0:T(8,128)(2,1)S(1)} %collective-permute-done.12), channel_id=1, source_target_pairs={{0,4},{1,3},{4,8},{5,1},{8,12},{9,5},{12,14},{13,9},{14,10},{15,13... | collective-permute-start | bytes 1179656 | tf_op jit(solution)/shard_map/hop_x/ppermute | solution.py:55
  48.1 14.6 %collective-permute-start.11 = (bf16[128,1536]{1,0:T(8,128)(2,1)S(1)}, bf16[128,1536]{1,0:T(8,128)(2,1)S(1)}, u32[]{:S(2)}, u32[]{:S(2)}) collective-permute-start(bf16[128,1536]{1,0:T(8,128)(2,1)S(1)} %collective-permute-done.8), channel_id=1, source_target_pairs={{0,4},{1,3},{4,8},{5,1},{8,12},{9,5},{12,14},{13,9},{14,10},{15,13... | collective-permute-start | bytes 1179656 | tf_op jit(solution)/shard_map/hop_g/ppermute | solution.py:55
  52.8 12.4 %collective-permute-start.16 = (bf16[128,1536]{1,0:T(8,128)(2,1)S(1)}, bf16[128,1536]{1,0:T(8,128)(2,1)S(1)}, u32[]{:S(2)}, u32[]{:S(2)}) collective-permute-start(bf16[128,1536]{1,0:T(8,128)(2,1)S(1)} %fusion.4), channel_id=1, source_target_pairs={{0,4},{1,3},{4,8},{5,1},{8,12},{9,5},{12,14},{13,9},{14,10},{15,13... | collective-permute-start | bytes 1179656 | tf_op jit(solution)/shard_map/hop_sum/ppermute | solution.py:55
  61.0 8.5 %collective-permute-start.18 = (bf16[128,1536]{1,0:T(8,128)(2,1)S(1)}, bf16[128,1536]{1,0:T(8,128)(2,1)S(1)}, u32[]{:S(2)}, u32[]{:S(2)}) collective-permute-start(bf16[128,1536]{1,0:T(8,128)(2,1)S(1)} %collective-permute-done.15), channel_id=1, source_target_pairs={{0,4},{1,3},{4,8},{5,1},{8,12},{9,5},{12,14},{13,9},{14,10},{15,13... | collective-permute-start | bytes 1179656 | tf_op jit(solution)/shard_map/hop_x/ppermute | solution.py:55
  62.7 10.7 %collective-permute-start.14 = (bf16[128,1536]{1,0:T(8,128)(2,1)S(1)}, bf16[128,1536]{1,0:T(8,128)(2,1)S(1)}, u32[]{:S(2)}, u32[]{:S(2)}) collective-permute-start(bf16[128,1536]{1,0:T(8,128)(2,1)S(1)} %collective-permute-done.11), channel_id=1, source_target_pairs={{0,4},{1,3},{4,8},{5,1},{8,12},{9,5},{12,14},{13,9},{14,10},{15,13... | collective-permute-start | bytes 1179656 | tf_op jit(solution)/shard_map/hop_g/ppermute | solution.py:55
  65.7 11.9 %collective-permute-start.19 = (bf16[128,1536]{1,0:T(8,128)(2,1)S(1)}, bf16[128,1536]{1,0:T(8,128)(2,1)S(1)}, u32[]{:S(2)}, u32[]{:S(2)}) collective-permute-start(bf16[128,1536]{1,0:T(8,128)(2,1)S(1)} %fusion.5), channel_id=1, source_target_pairs={{0,4},{1,3},{4,8},{5,1},{8,12},{9,5},{12,14},{13,9},{14,10},{15,13... | collective-permute-start | bytes 1179656 | tf_op jit(solution)/shard_map/hop_sum/ppermute | solution.py:55
  69.5 12.5 %collective-permute-start.20 = (bf16[128,1536]{1,0:T(8,128)(2,1)S(1)}, bf16[128,1536]{1,0:T(8,128)(2,1)S(1)}, u32[]{:S(2)}, u32[]{:S(2)}) collective-permute-start(bf16[128,1536]{1,0:T(8,128)(2,1)S(1)} %collective-permute-done.18), channel_id=1, source_target_pairs={{0,4},{1,3},{4,8},{5,1},{8,12},{9,5},{12,14},{13,9},{14,10},{15,13... | collective-permute-start | bytes 1179656 | tf_op jit(solution)/shard_map/hop_x/ppermute | solution.py:55
  73.3 12.6 %collective-permute-start.17 = (bf16[128,1536]{1,0:T(8,128)(2,1)S(1)}, bf16[128,1536]{1,0:T(8,128)(2,1)S(1)}, u32[]{:S(2)}, u32[]{:S(2)}) collective-permute-start(bf16[128,1536]{1,0:T(8,128)(2,1)S(1)} %collective-permute-done.14), channel_id=1, source_target_pairs={{0,4},{1,3},{4,8},{5,1},{8,12},{9,5},{12,14},{13,9},{14,10},{15,13... | collective-permute-start | bytes 1179656 | tf_op jit(solution)/shard_map/hop_g/ppermute | solution.py:55
  77.9 10.2 %collective-permute-start.21 = (bf16[128,768]{1,0:T(8,128)(2,1)S(1)}, bf16[128,768]{1,0:T(8,128)(2,1)S(1)}, u32[]{:S(2)}, u32[]{:S(2)}) collective-permute-start(bf16[128,768]{1,0:T(8,128)(2,1)S(1)} %fusion.6), channel_id=1, source_target_pairs={{0,4},{1,3},{4,8},{5,1},{8,12},{9,5},{12,14},{13,9},{14,10},{15,13... | collective-permute-start | bytes 589832 | tf_op jit(solution)/shard_map/hop_sum/ppermute | solution.py:55
  80.4 10.2 %collective-permute-start.23 = (bf16[128,768]{1,0:T(8,128)(2,1)S(1)}, bf16[128,768]{1,0:T(8,128)(2,1)S(1)}, u32[]{:S(2)}, u32[]{:S(2)}) collective-permute-start(bf16[128,768]{1,0:T(8,128)(2,1)S(1)} %fusion.7), channel_id=1, source_target_pairs={{0,4},{1,3},{4,8},{5,1},{8,12},{9,5},{12,14},{13,9},{14,10},{15,13... | collective-permute-start | bytes 589832 | tf_op jit(solution)/shard_map/hop_sum/ppermute | solution.py:55
  88.1 6.1 %collective-permute-start.25 = (bf16[384,1536]{1,0:T(8,128)(2,1)S(1)}, bf16[384,1536]{1,0:T(8,128)(2,1)S(1)}, u32[]{:S(2)}, u32[]{:S(2)}) collective-permute-start(bf16[384,1536]{1,0:T(8,128)(2,1)S(1)} %fusion), channel_id=1, source_target_pairs={{0,1},{1,0},{2,3},{3,2},{4,5},{5,4},{6,7},{7,6},{8,9},{9,8},{10,11... | collective-permute-start | bytes 3538952 | tf_op jit(solution)/shard_map/swap_grads/ppermute | solution.py:59
  88.4 5.7 %collective-permute-start.22 = (bf16[128,768]{1,0:T(8,128)(2,1)S(1)}, bf16[128,768]{1,0:T(8,128)(2,1)S(1)}, u32[]{:S(2)}, u32[]{:S(2)}) collective-permute-start(bf16[128,768]{1,0:T(8,128)(2,1)S(1)} %fusion.8), channel_id=1, source_target_pairs={{0,4},{1,3},{4,8},{5,1},{8,12},{9,5},{12,14},{13,9},{14,10},{15,13... | collective-permute-start | bytes 589832 | tf_op jit(solution)/shard_map/hop_sum/ppermute | solution.py:55
  90.6 5.3 %collective-permute-start.26 = (bf16[384,1536]{1,0:T(8,128)(2,1)S(1)}, bf16[384,1536]{1,0:T(8,128)(2,1)S(1)}, u32[]{:S(2)}, u32[]{:S(2)}) collective-permute-start(bf16[384,1536]{1,0:T(8,128)(2,1)S(1)} %fusion.1), channel_id=1, source_target_pairs={{0,1},{1,0},{2,3},{3,2},{4,5},{5,4},{6,7},{7,6},{8,9},{9,8},{10,11... | collective-permute-start | bytes 3538952 | tf_op jit(solution)/shard_map/swap_grads/ppermute | solution.py:59
  91.6 6.1 %collective-permute-start.24 = (bf16[128,768]{1,0:T(8,128)(2,1)S(1)}, bf16[128,768]{1,0:T(8,128)(2,1)S(1)}, u32[]{:S(2)}, u32[]{:S(2)}) collective-permute-start(bf16[128,768]{1,0:T(8,128)(2,1)S(1)} %fusion.9), channel_id=1, source_target_pairs={{0,4},{1,3},{4,8},{5,1},{8,12},{9,5},{12,14},{13,9},{14,10},{15,13... | collective-permute-start | bytes 589832 | tf_op jit(solution)/shard_map/hop_sum/ppermute | solution.py:55
